TPU v7x, 32 devices: a whole 2x2x4 slice. The times are simulated.
32 devices in a mesh: groups: 2 (over y), ctx: 4 (over z), dp: 2 (over x), mp: 2 (over core).
Axes of the slice: x: 2, y: 2, z: 4, core: 2. Of those that a mesh axis runs over, the one named last changes fastest.
Arguments:
- queries: bfloat16 [4, 2048, 1024], P(('groups', 'dp'), 'ctx', 'mp'), parts along dimension 0, may hold values from -6 to 6
- key_vectors: bfloat16 [4, 2048, 1024], P(('groups', 'dp'), 'ctx', 'mp'), parts along dimension 0, may hold values from -1.1953125 to 1.1953125
- value_vectors: bfloat16 [4, 2048, 2048], P(('groups', 'dp'), 'ctx', 'mp'), parts along dimension 0, may hold values from -6 to 6
- log_gates: bfloat16 [4, 2048, 1024], P(('groups', 'dp'), 'ctx', 'mp'), parts along dimension 0, may hold values from -1 to 0
- doc_lengths: int32 [4, 6], P(('groups', 'dp')), parts along dimension 0, may hold values from 1 to 1024, 2048 in all within a row
- cotangent: bfloat16 [4, 2048, 2048], P(('groups', 'dp'), 'ctx'), parts along dimension 0, may hold values from -0.59765625 to 0.59765625
- out_weight: bfloat16 [2048, 2048], P('mp'), may hold values from -0.125 to 0.125
Outputs:
- query_grad: bfloat16 [4, 2048, 1024], P(('groups', 'dp'), 'ctx', 'mp'), parts along dimension 0
- key_grad: bfloat16 [4, 2048, 1024], P(('groups', 'dp'), 'ctx', 'mp'), parts along dimension 0
- value_grad: bfloat16 [4, 2048, 2048], P(('groups', 'dp'), 'ctx', 'mp'), parts along dimension 0
- projection_weight_gradient: float32 [4096, 2048], P(('groups', 'mp'), ('ctx', 'dp')), parts along dimension 0
There are 2 independent parts, one for each index of `groups`. A program takes and returns all parts, laid end to end along the dimension named above; an argument that names none is the same for every part. Nothing has to cross between parts.
Inputs may be any that keep to these rules, and one draw needn't show every extreme that they name: `doc_lengths`: the lengths of one sequence's documents sum to 2048; the longest is 1024.
All inputs are finite; a program needn't handle non-finite values.
Results may differ from a plain program's by a relative error of at most 0.0029.
Values sent between devices are 32-bit elements; how exact they have to be, the bound alone decides.
A program may use at most 128 MiB of HBM per device.

v0:
```python
import functools
import math

import jax
import jax.numpy as jnp
from jax import lax
from jax.experimental import pallas as pl
from jax.experimental.pallas import tpu as pltpu
from jax.sharding import PartitionSpec as P

KEY = 256
VAL = 512
SPAN = 128
SCALE = KEY ** (-0.5)
VMEM_BYTES = 48 * 1024 * 1024
MESH = pl.DeviceIdType.MESH
F32 = jnp.float32
BF16 = jnp.bfloat16

NN = (((1,), (0,)), ((), ()))
NT = (((1,), (1,)), ((), ()))
TN = (((0,), (0,)), ((), ()))


def dot(a, b, dims):
    return lax.dot_general(a, b, dims, preferred_element_type=F32)


def split(x):
    high = x.astype(BF16)
    return high, (x - high.astype(F32)).astype(BF16)


def whole(x):
    return x, None


def product(a, b, dims):
    out = dot(a[0], b[0], dims)
    if a[1] is not None:
        out = out + dot(a[1], b[0], dims)
    if b[1] is not None:
        out = out + dot(a[0], b[1], dims)
    return out


def bounds_of(lens_ref):
    bounds, total = [], 0
    for d in range(lens_ref.shape[1]):
        total = total + lens_ref[0, d]
        bounds.append(total)
    return bounds


def doc_scalar(bounds, position):
    count = jnp.int32(0)
    for bound in bounds:
        count = count + jnp.where(position >= bound, 1, 0).astype(jnp.int32)
    return count


def doc_array(bounds, first, shape, dim):
    positions = first + lax.broadcasted_iota(jnp.int32, shape, dim)
    count = jnp.zeros(shape, jnp.int32)
    for bound in bounds:
        count = count + jnp.where(positions >= bound, 1, 0)
    return count


def alive_and_trailing(bounds, first, rows, columns):
    docs = doc_array(bounds, first, (rows, columns), 0)
    before = jnp.where(first > 0, doc_scalar(bounds, first - 1), -1)
    last = doc_scalar(bounds, first + rows - 1)
    living = jnp.where(docs == before, 1.0, 0.0).astype(F32)
    trailing = jnp.where(docs == last, 1.0, 0.0).astype(F32)
    return living, trailing


def running_sum(gates):
    rows = gates.shape[0]
    lower = lax.broadcasted_iota(jnp.int32, (rows, rows), 0) >= lax.broadcasted_iota(
        jnp.int32, (rows, rows), 1
    )
    return dot(jnp.where(lower, 1.0, 0.0).astype(BF16), gates, NN)


def states_kernel(lens, q, k, v, gates, cot, weight, grad_o, fwd_o, bwd_o, decay_o):
    tokens = q.shape[0]
    bounds = bounds_of(lens)
    first = lax.axis_index("ctx") * tokens
    grad = dot(cot[...], weight[...], NT)
    grad_o[...] = grad
    cumulative = running_sum(gates[...])
    end = cumulative[tokens - 1 :, :]
    living, trailing = alive_and_trailing(bounds, first, tokens, KEY)
    tail = k[...].astype(F32) * jnp.exp(end - cumulative) * trailing
    alive = q[...].astype(F32) * SCALE * jnp.exp(cumulative) * living
    fwd_o[...] = product(whole(v[...]), split(tail), TN)
    bwd_o[...] = product(split(grad), split(alive), TN)
    decay_o[...] = (jnp.exp(end) * living[tokens - 1 :, :])[None]


def chain_kernel(n, pieces, fwd, bwd, decay, fwd_in, bwd_in, f_send, b_send, f_recv, b_recv, sems):
    me = lax.axis_index("ctx")
    rows = fwd.shape[0] // pieces
    per_head = pieces // decay.shape[0]
    has_left, has_right = me > 0, me < n - 1
    barrier = pltpu.get_barrier_semaphore()

    @pl.when(has_left)
    def _():
        pl.semaphore_signal(barrier, inc=1, device_id={"ctx": me - 1}, device_id_type=MESH)

    @pl.when(has_right)
    def _():
        pl.semaphore_signal(barrier, inc=1, device_id={"ctx": me + 1}, device_id_type=MESH)

    pl.semaphore_wait(barrier, has_left.astype(jnp.int32) + has_right.astype(jnp.int32))

    def copy_of(c, send, recv, base, to):
        at = pl.ds(pl.multiple_of(c * rows, rows), rows)
        return pltpu.make_async_remote_copy(
            src_ref=send.at[at],
            dst_ref=recv.at[at],
            send_sem=sems.at[base, c],
            recv_sem=sems.at[base + 1, c],
            device_id={"ctx": to},
            device_id_type=MESH,
        )

    def one(c, own, send, recv, result, base, has_source, has_target, to):
        at = pl.ds(pl.multiple_of(c * rows, rows), rows)

        @pl.when(has_source)
        def _():
            copy_of(c, send, recv, base, to).wait_recv()
            result[at, :] = recv[at, :]

        @pl.when(jnp.logical_not(has_source))
        def _():
            result[at, :] = jnp.zeros((rows, KEY), F32)

        @pl.when(has_target)
        def _():
            send[at, :] = decay[c // per_head] * result[at, :] + own[at, :]
            copy_of(c, send, recv, base, to).start()

    right = jnp.minimum(me + 1, n - 1)
    left = jnp.maximum(me - 1, 0)

    def slot(s, carry):
        up = s - me
        down = s - (n - 1 - me)

        @pl.when((up >= 0) & (up < pieces))
        def _():
            one(up, fwd, f_send, f_recv, fwd_in, 0, has_left, has_right, right)

        @pl.when((down >= 0) & (down < pieces))
        def _():
            one(down, bwd, b_send, b_recv, bwd_in, 2, has_right, has_left, left)

        return carry

    lax.fori_loop(0, pieces + n - 1, slot, 0)

    def finish(c, carry):
        @pl.when(has_right)
        def _():
            copy_of(c, f_send, f_recv, 0, right).wait_send()

        @pl.when(has_left)
        def _():
            copy_of(c, b_send, b_recv, 2, left).wait_send()

        return carry

    lax.fori_loop(0, pieces, finish, 0)


def outputs_kernel(lens, q, k, v, gates, grad, fwd, bwd, *rest):
    q_o, k_o, v_o, attn_o, scores_s, mixing_s, grown_s, cum_s = rest[-8:]
    tokens = q.shape[0]
    blocks = tokens // SPAN
    bounds = bounds_of(lens)
    device_first = lax.axis_index("ctx") * tokens
    state = fwd[...]
    for n in range(blocks):
        at = slice(n * SPAN, (n + 1) * SPAN)
        first = device_first + n * SPAN
        cumulative = running_sum(gates[at, :])
        cum_s[at, :] = cumulative
        growth = jnp.exp(cumulative)
        shrink = jnp.exp(-cumulative)
        end = cumulative[SPAN - 1 :, :]
        living, trailing = alive_and_trailing(bounds, first, SPAN, KEY)
        rows = lax.broadcasted_iota(jnp.int32, (SPAN, SPAN), 0)
        columns = lax.broadcasted_iota(jnp.int32, (SPAN, SPAN), 1)
        same = doc_array(bounds, first, (SPAN, SPAN), 0) == doc_array(bounds, first, (SPAN, SPAN), 1)
        mask = jnp.where((rows >= columns) & same, 1.0, 0.0).astype(F32)
        value = whole(v[at, :])
        key = k[at, :].astype(F32)
        grown = q[at, :].astype(F32) * SCALE * growth
        grown_s[at, :] = grown
        shrunk = key * shrink
        grown_p, shrunk_p, grad_p = split(grown), split(shrunk), split(grad[at, :])
        scores = product(grown_p, shrunk_p, NT) * mask
        mixing = product(grad_p, value, NT) * mask
        scores_s[at, :] = scores
        mixing_s[at, :] = mixing
        state_p = split(state)
        alive = split(grown * living)
        out = product(split(scores), value, NN) + product(alive, state_p, NT)
        attn_o[at, :] = out.astype(BF16).astype(F32)
        dq = product(split(mixing), shrunk_p, NN) + living * product(grad_p, state_p, NN)
        q_o[at, :] = (growth * dq * SCALE).astype(BF16)
        if n < blocks - 1:
            tail = split(key * jnp.exp(end - cumulative) * trailing)
            decay = jnp.exp(end) * living[SPAN - 1 :, :]
            state = decay * state + product(value, tail, TN)
    state = bwd[...]
    for n in reversed(range(blocks)):
        at = slice(n * SPAN, (n + 1) * SPAN)
        first = device_first + n * SPAN
        cumulative = cum_s[at, :]
        shrink = jnp.exp(-cumulative)
        end = cumulative[SPAN - 1 :, :]
        living, trailing = alive_and_trailing(bounds, first, SPAN, KEY)
        value = whole(v[at, :])
        grad_p = split(grad[at, :])
        grown = grown_s[at, :]
        from_end = jnp.exp(end - cumulative) * trailing
        tail = split(k[at, :].astype(F32) * from_end)
        state_p = split(state)
        dk = shrink * product(split(mixing_s[at, :]), split(grown), TN)
        dk = dk + from_end * product(value, state_p, NN)
        k_o[at, :] = dk.astype(BF16)
        dv = product(split(scores_s[at, :]), grad_p, TN) + product(tail, state_p, NT)
        v_o[at, :] = dv.astype(BF16)
        if n > 0:
            decay = jnp.exp(end) * living[SPAN - 1 :, :]
            state = decay * state + product(grad_p, split(grown * living), TN)


def weight_kernel(peers, norm, *refs):
    out = refs[-1]
    total = None
    for p in range(peers):
        term = dot(refs[p][...].astype(BF16), refs[peers + p][0].astype(BF16), TN)
        total = term if total is None else total + term
    out[...] = (total * norm)[None]


def params(**more):
    return pltpu.CompilerParams(vmem_limit_bytes=VMEM_BYTES, **more)


def per_device(queries, key_vectors, value_vectors, log_gates, doc_lengths, cotangent, out_weight):
    q, k, v, gates, cot = (x[0] for x in (queries, key_vectors, value_vectors, log_gates, cotangent))
    tokens, width = cot.shape
    heads = out_weight.shape[0] // VAL
    n, peers = lax.axis_size("ctx"), lax.axis_size("dp")
    dp = lax.axis_index("dp")
    columns = width // (n * peers)
    smem = pl.BlockSpec(memory_space=pltpu.SMEM)

    parted = cot.reshape(tokens, n, peers, columns)

    def part_for(p):
        return lax.dynamic_index_in_dim(parted, p, axis=2, keepdims=False).transpose(1, 0, 2)

    def shift(x, s):
        return lax.ppermute(x, "dp", [(i, (i + s) % peers) for i in range(peers)])

    cots = [part_for(dp)]
    for s in range(1, peers):
        cots.append(shift(part_for(lax.rem(dp + s, peers)).astype(F32), s))

    def head_block(rows, cols):
        return pl.BlockSpec((rows, cols), lambda h: (0, h))

    def head_rows(rows, cols):
        return pl.BlockSpec((rows, cols), lambda h: (h, 0))

    grad, fwd, bwd, decay = pl.pallas_call(
        states_kernel,
        grid=(heads,),
        in_specs=[
            smem,
            head_block(tokens, KEY),
            head_block(tokens, KEY),
            head_block(tokens, VAL),
            head_block(tokens, KEY),
            pl.BlockSpec((tokens, width), lambda h: (0, 0)),
            head_rows(VAL, width),
        ],
        out_specs=[
            head_block(tokens, VAL),
            head_rows(VAL, KEY),
            head_rows(VAL, KEY),
            pl.BlockSpec((1, 1, KEY), lambda h: (h, 0, 0)),
        ],
        out_shape=[
            jax.ShapeDtypeStruct((tokens, heads * VAL), F32),
            jax.ShapeDtypeStruct((heads * VAL, KEY), F32),
            jax.ShapeDtypeStruct((heads * VAL, KEY), F32),
            jax.ShapeDtypeStruct((heads, 1, KEY), F32),
        ],
        compiler_params=params(),
        cost_estimate=pl.CostEstimate(flops=6 * 10**9, bytes_accessed=14 << 20, transcendentals=0),
        name="states",
    )(doc_lengths, q, k, v, gates, cot, out_weight)

    pieces = 8 * heads
    vmem = pl.BlockSpec(memory_space=pltpu.VMEM)
    state_shape = (heads * VAL, KEY)
    fwd_in, bwd_in = pl.pallas_call(
        functools.partial(chain_kernel, n, pieces),
        in_specs=[vmem] * 3,
        out_specs=[vmem] * 2,
        out_shape=[jax.ShapeDtypeStruct(state_shape, F32)] * 2,
        scratch_shapes=[pltpu.VMEM(state_shape, F32)] * 4 + [pltpu.SemaphoreType.DMA((4, pieces))],
        compiler_params=params(collective_id=0, has_side_effects=True),
        cost_estimate=pl.CostEstimate(flops=10**6, bytes_accessed=64 << 20, transcendentals=0),
        name="chain",
    )(fwd, bwd, decay)

    grads = []
    attn = []
    for h in range(heads):
        def cols(c, h=h):
            return pl.BlockSpec((tokens, c), lambda i: (0, h))

        def state_rows(h=h):
            return pl.BlockSpec((VAL, KEY), lambda i: (h, 0))

        results = pl.pallas_call(
            outputs_kernel,
            grid=(1,),
            in_specs=[smem, cols(KEY), cols(KEY), cols(VAL), cols(KEY), cols(VAL)]
            + [state_rows()] * 2
            + [pl.BlockSpec(memory_space=pl.ANY)] * len(grads),
            out_specs=[
                cols(KEY),
                cols(KEY),
                cols(VAL),
                pl.BlockSpec((tokens, VAL), lambda i: (0, 0)),
            ],
            out_shape=[
                jax.ShapeDtypeStruct((tokens, heads * KEY), BF16),
                jax.ShapeDtypeStruct((tokens, heads * KEY), BF16),
                jax.ShapeDtypeStruct((tokens, heads * VAL), BF16),
                jax.ShapeDtypeStruct((tokens, VAL), F32),
            ],
            scratch_shapes=[
                pltpu.VMEM((tokens, SPAN), F32),
                pltpu.VMEM((tokens, SPAN), F32),
                pltpu.VMEM((tokens, KEY), F32),
                pltpu.VMEM((tokens, KEY), F32),
            ],
            input_output_aliases={8 + i: i for i in range(len(grads))},
            compiler_params=params(),
            cost_estimate=pl.CostEstimate(flops=3 * 10**9, bytes_accessed=8 << 20, transcendentals=0),
            name="outputs",
        )(doc_lengths, q, k, v, gates, grad, fwd_in, bwd_in, *grads)
        grads = list(results[:3])
        attn.append(results[3])

    norm = 1.0 / math.sqrt(peers * n * tokens)
    sums = []
    for h in range(heads):
        everyone = [attn[h]] + [shift(attn[h], s) for s in range(1, peers)]
        partial = pl.pallas_call(
            functools.partial(weight_kernel, peers, norm),
            grid=(n,),
            in_specs=[pl.BlockSpec((tokens, VAL), lambda c: (0, 0))] * peers
            + [pl.BlockSpec((1, tokens, columns), lambda c: (c, 0, 0))] * peers,
            out_specs=pl.BlockSpec((1, VAL, columns), lambda c: (c, 0, 0)),
            out_shape=jax.ShapeDtypeStruct((n, VAL, columns), F32),
            compiler_params=params(),
            cost_estimate=pl.CostEstimate(flops=2 * 10**9, bytes_accessed=8 << 20, transcendentals=0),
            name="weight",
        )(*everyone, *cots)
        sums.append(lax.psum_scatter(partial, "ctx", scatter_dimension=0, tiled=True)[0])
    weight_grad = jnp.concatenate(sums, axis=0)
    return (grads[0][None], grads[1][None], grads[2][None], weight_grad)


def solution(mesh):
    batch = ("groups", "dp")
    return jax.shard_map(
        per_device,
        mesh=mesh,
        in_specs=(
            P(batch, "ctx", "mp"),
            P(batch, "ctx", "mp"),
            P(batch, "ctx", "mp"),
            P(batch, "ctx", "mp"),
            P(batch, None),
            P(batch, "ctx", None),
            P("mp", None),
        ),
        out_specs=(
            P(batch, "ctx", "mp"),
            P(batch, "ctx", "mp"),
            P(batch, "ctx", "mp"),
            P(("groups", "mp"), ("ctx", "dp")),
        ),
        check_vma=False,
    )
```

profile of v0, /device:TPU:0, one launch (start us, length us, event | category | flops | bytes accessed | tf_op | source)
XLA Modules:
  0.0 220.0 jit_solution(5216281891971621871)
XLA Ops:
  7.2 0.0 reduce-scatter.5.cloned.1.call-start
  7.2 2.9 %copy.14 = bf16[1,512,2048]{1,2,0:T(8,128)(2,1)S(1)} copy(bf16[1,512,2048]{2,1,0:T(8,128)(2,1)} %param.12) | data formatting | bytes 4194304 | tf_op args[5]
  10.1 1.2 constant_dynamic-slice_fusion
  11.3 0.5 copy.17
  11.8 0.0 copy-start
  11.8 0.0 copy-start.1
  11.8 0.0 copy-start.2
  11.8 0.0 copy-start.3
  11.8 0.0 copy-start.4
  11.9 1.5 convert_bitcast_fusion
  13.4 2.9 %collective-permute-start.1 = (f32[4,512,256]{2,1,0:T(8,128)}, f32[4,512,256]{2,1,0:T(8,128)}, u32[]{:S(2)}, u32[]{:S(2)}) collective-permute-start(f32[4,512,256]{2,1,0:T(8,128)} %convert_bitcast_fusion), channel_id=1, source_target_pairs={{0,2},{2,0},{1,3},{3,1},{4,6},{6,4},{5,7},{7,5},{8,10},{10,8},{9,1... | collective-permute-start | bytes 6291464 | tf_op jit(solution)/shard_map/ppermute | solution.py:273
  16.3 0.0 copy-done
  16.3 0.0 copy-done.1
  16.3 0.0 copy-done.2
  16.3 0.0 copy-done.3
  16.3 0.0 copy-done.4
  16.3 7.7 %states.1 = (f32[512,1024]{1,0:T(8,128)}, f32[1024,256]{1,0:T(8,128)S(1)}, f32[1024,256]{1,0:T(8,128)S(1)}, f32[2,1,256]{2,1,0:T(1,128)S(1)}) custom-call(s32[1,6]{1,0:T(1,128)S(1)} %copy-done.4, bf16[512,512]{1,0:T(8,128)(2,1)S(1)} %bitcast.24, bf16[512,512]{1,0:T(8,128)(2,1)S(1)} %bitcast.27, bf16[512,1024]{1,0:T(8,128)(2,1)S(1)} %bitcast.21, ...), custom_call_target="tpu_custom_call" | custom-call | flops 6000000000 | bytes 14680064 | tf_op jit(solution)/shard_map/states/pallas_call | solution.py:285
  24.0 58.8 %chain.1 = (f32[1024,256]{1,0:T(8,128)S(1)}, f32[1024,256]{1,0:T(8,128)S(1)}) custom-call(f32[1024,256]{1,0:T(8,128)S(1)} %get-tuple-element.19.fwd, f32[1024,256]{1,0:T(8,128)S(1)} %get-tuple-element.20.bwd, f32[2,1,256]{2,1,0:T(1,128)S(1)} %get-tuple-element.21.decay), custom_call_target="tpu_custom_call" | custom-call | flops 1000000 | bytes 67108864 | tf_op jit(solution)/shard_map/chain/pallas_call | solution.py:317
  82.8 9.0 %outputs.2 = (bf16[512,512]{1,0:T(8,128)(2,1)}, bf16[512,512]{1,0:T(8,128)(2,1)}, bf16[512,1024]{1,0:T(8,128)(2,1)}, f32[512,512]{1,0:T(8,128)S(1)}) custom-call(s32[1,6]{1,0:T(1,128)S(1)} %copy-done.4, bf16[512,512]{1,0:T(8,128)(2,1)S(1)} %bitcast.25, bf16[512,512]{1,0:T(8,128)(2,1)S(1)} %bitcast.28, bf16[512,1024]{1,0:T(8,128)(2,1)S(1)} %bitcast.22, ...), custom_call_target="tpu_custom_call" | custom-call | flops 3000000000 | bytes 8388608 | tf_op jit(solution)/shard_map/outputs/pallas_call | solution.py:337
  91.8 9.0 %outputs.3 = (bf16[512,512]{1,0:T(8,128)(2,1)}, bf16[512,512]{1,0:T(8,128)(2,1)}, bf16[512,1024]{1,0:T(8,128)(2,1)}, f32[512,512]{1,0:T(8,128)S(1)}) custom-call(s32[1,6]{1,0:T(1,128)S(1)} %copy-done.4, bf16[512,512]{1,0:T(8,128)(2,1)S(1)} %bitcast.26, bf16[512,512]{1,0:T(8,128)(2,1)S(1)} %bitcast.29, ...), custom_call_target="tpu_custom_call", output_to_operand_aliasing={{0}: (8, {}), {1}: (9, {}), {2}: (10, {})} | custom-call | flops 3000000000 | bytes 8388608 | tf_op jit(solution)/shard_map/outputs/pallas_call | solution.py:337
  100.7 0.3 collective-permute-start.2
  101.0 1.5 copy.15
  102.5 16.4 %collective-permute-done.2.refs_1_ = f32[512,512]{1,0:T(8,128)} collective-permute-done((f32[512,512]{1,0:T(8,128)S(1)}, f32[512,512]{1,0:T(8,128)}, u32[]{:S(2)}, u32[]{:S(2)}) %collective-permute-start.2) | collective-permute-done | bytes 1048608 | tf_op jit(solution)/shard_map/ppermute | solution.py:273
  118.8 0.0 collective-permute-done.1.refs_3_
  118.9 5.0 %weight.5 = f32[4,512,256]{2,1,0:T(8,128)} custom-call(f32[512,512]{1,0:T(8,128)S(1)} %get-tuple-element.31.refs_0_, f32[512,512]{1,0:T(8,128)} %collective-permute-done.2.refs_1_, bf16[4,512,256]{2,1,0:T(8,128)(2,1)S(1)} %bitcast.19, f32[4,512,256]{2,1,0:T(8,128)} %collective-permute-done.1.refs_3_), custom_call_target="tpu_custom_call" | custom-call | flops 2000000000 | bytes 8388608 | tf_op jit(solution)/shard_map/weight/pallas_call | solution.py:373
  123.9 0.0 reduce-scatter.5.cloned.1.call-update
  123.9 0.0 reduce-scatter.3.cloned.1.call-start
  124.0 0.3 collective-permute-start
  124.3 14.5 %collective-permute-done.refs_1_ = f32[512,512]{1,0:T(8,128)S(1)} collective-permute-done((f32[512,512]{1,0:T(8,128)S(1)}, f32[512,512]{1,0:T(8,128)S(1)}, u32[]{:S(2)}, u32[]{:S(2)}) %collective-permute-start) | collective-permute-done | bytes 1048608 | tf_op jit(solution)/shard_map/ppermute | solution.py:273
  138.8 4.7 %weight.4 = f32[4,512,256]{2,1,0:T(8,128)} custom-call(f32[512,512]{1,0:T(8,128)S(1)} %get-tuple-element.30.refs_0_, f32[512,512]{1,0:T(8,128)S(1)} %collective-permute-done.refs_1_, bf16[4,512,256]{2,1,0:T(8,128)(2,1)S(1)} %bitcast.20, f32[4,512,256]{2,1,0:T(8,128)} %collective-permute-done.1.refs_3_), custom_call_target="tpu_custom_call" | custom-call | flops 2000000000 | bytes 8388608 | tf_op jit(solution)/shard_map/weight/pallas_call | solution.py:373
  143.5 0.0 reduce-scatter.3.cloned.1.call-update
  143.6 21.8 %reduce-scatter.5.cloned.1.call-done = f32[1,512,256]{2,1,0:T(8,128)} async-done(((f32[4,512,256]{2,1,0:T(8,128)}), f32[1,512,256]{2,1,0:T(8,128)}) %reduce-scatter.5.cloned.1.call-update) | async-done | bytes 524304 | tf_op jit(solution)/shard_map/reduce_scatter | solution.py:384
  165.3 45.6 %reduce-scatter.3.cloned.1.call-done = f32[1,512,256]{2,1,0:T(8,128)} async-done(((f32[4,512,256]{2,1,0:T(8,128)}), f32[1,512,256]{2,1,0:T(8,128)}) %reduce-scatter.3.cloned.1.call-update) | async-done | bytes 524304 | tf_op jit(solution)/shard_map/reduce_scatter | solution.py:384
  211.0 2.2 %pad_maximum_fusion = f32[1024,256]{1,0:T(8,128)} fusion(f32[512,256]{1,0:T(8,128)} %bitcast.35, f32[512,256]{1,0:T(8,128)} %bitcast.36), kind=kLoop, calls=%fused_computation.1 | loop fusion | flops 262144 | bytes 2097152 | tf_op jit(solution)/shard_map/concatenate | solution.py:385
Async XLA Ops:
  7.2 158.2 %reduce-scatter.5.cloned.1.call-start = ((), (), s32[]{:S(2)}) async-start(), calls=%async_computation.3 | async-start | bytes 2621440 | tf_op jit(solution)/shard_map/reduce_scatter | solution.py:384
  11.8 4.5 %copy-start = (bf16[1,512,1024]{2,1,0:T(8,128)(2,1)S(1)}, bf16[1,512,1024]{2,1,0:T(8,128)(2,1)}, u32[]{:S(2)}) copy-start(bf16[1,512,1024]{2,1,0:T(8,128)(2,1)} %param.9) | copy-start | bytes 3145732
  11.8 4.5 %copy-start.1 = (bf16[1,512,512]{2,1,0:T(8,128)(2,1)S(1)}, bf16[1,512,512]{2,1,0:T(8,128)(2,1)}, u32[]{:S(2)}) copy-start(bf16[1,512,512]{2,1,0:T(8,128)(2,1)} %param.7) | copy-start | bytes 1572868
  11.8 4.5 %copy-start.2 = (bf16[1,512,512]{2,1,0:T(8,128)(2,1)S(1)}, bf16[1,512,512]{2,1,0:T(8,128)(2,1)}, u32[]{:S(2)}) copy-start(bf16[1,512,512]{2,1,0:T(8,128)(2,1)} %param.8) | copy-start | bytes 1572868
  11.8 4.5 %copy-start.3 = (bf16[1,512,512]{2,1,0:T(8,128)(2,1)S(1)}, bf16[1,512,512]{2,1,0:T(8,128)(2,1)}, u32[]{:S(2)}) copy-start(bf16[1,512,512]{2,1,0:T(8,128)(2,1)} %param.10) | copy-start | bytes 1572868
  11.8 4.5 %copy-start.4 = (s32[1,6]{1,0:T(1,128)S(1)}, s32[1,6]{1,0:T(1,128)}, u32[]{:S(2)}) copy-start(s32[1,6]{1,0:T(1,128)} %lens.5) | copy-start | bytes 76
  13.4 105.5 %collective-permute-start.1 = (f32[4,512,256]{2,1,0:T(8,128)}, f32[4,512,256]{2,1,0:T(8,128)}, u32[]{:S(2)}, u32[]{:S(2)}) collective-permute-start(f32[4,512,256]{2,1,0:T(8,128)} %convert_bitcast_fusion), channel_id=1, source_target_pairs={{0,2},{2,0},{1,3},{3,1},{4,6},{6,4},{5,7},{7,5},{8,10},{10,8},{9,1... | collective-permute-start | bytes 6291464 | tf_op jit(solution)/shard_map/ppermute | solution.py:273
  100.7 18.1 %collective-permute-start.2 = (f32[512,512]{1,0:T(8,128)S(1)}, f32[512,512]{1,0:T(8,128)}, u32[]{:S(2)}, u32[]{:S(2)}) collective-permute-start(f32[512,512]{1,0:T(8,128)S(1)} %get-tuple-element.31.refs_0_), channel_id=1, source_target_pairs={{0,2},{2,0},{1,3},{3,1},{4,6},{6,4},{5,7},{7,5},{8,10},{10,8},{9,1... | collective-permute-start | bytes 3145736 | tf_op jit(solution)/shard_map/ppermute | solution.py:273
  123.9 87.0 %reduce-scatter.3.cloned.1.call-start = ((), (), s32[]{:S(2)}) async-start(), calls=%async_computation.2 | async-start | bytes 2621440 | tf_op jit(solution)/shard_map/reduce_scatter | solution.py:384
  124.0 14.9 %collective-permute-start = (f32[512,512]{1,0:T(8,128)S(1)}, f32[512,512]{1,0:T(8,128)S(1)}, u32[]{:S(2)}, u32[]{:S(2)}) collective-permute-start(f32[512,512]{1,0:T(8,128)S(1)} %get-tuple-element.30.refs_0_), channel_id=1, source_target_pairs={{0,2},{2,0},{1,3},{3,1},{4,6},{6,4},{5,7},{7,5},{8,10},{10,8},{9,1... | collective-permute-start | bytes 3145736 | tf_op jit(solution)/shard_map/ppermute | solution.py:273
Sparse Core Ops, SparseCore 0:
  124.0 41.2 reduce-scatter.4
  167.7 43.1 reduce-scatter.2
where the time goes:
time: 220 us
  waiting for transfers between devices  98.3 us (45%)
  Pallas kernels  94.1 us (43%)
  between operations  14.1 us (6%)
  local copies, waits for them, and re-layouts  6.06 us (3%)
  other arithmetic  3.73 us (2%)
  starting transfers between devices  3.63 us (2%)
    reduce_scatter x2, waiting for transfers between devices, per_device(): lax.psum_scatter(partial, 'ctx', scatter_dimension=0, tiled=True)[0]  67.4 us
    pallas_call x1, Pallas kernels, per_device(): pl.pallas_call(functools.partial(chain_kernel, n, pieces), in_specs=[vmem...  58.8 us
    ppermute x3, waiting for transfers between devices, shift(): return lax.ppermute(x, 'dp', [(i, (i + s) % peers) for i in range(peers)])  30.9 us
    pallas_call x2, Pallas kernels, per_device(): pl.pallas_call(outputs_kernel, grid=(1,), in_specs=[smem, cols(KEY), cols...  17.9 us
    pallas_call x2, Pallas kernels, per_device(): pl.pallas_call(functools.partial(weight_kernel, peers, norm), grid=(n,),...  9.74 us
    pallas_call x1, Pallas kernels, per_device(): pl.pallas_call(states_kernel, grid=(heads,), in_specs=[smem, head_block(t...  7.65 us
  transfers between devices with their start and end apart: 5, of which 4 were waited for; matrix products, arithmetic and copies ran while one was open for 1% of the time, Pallas kernels for 40%

commit v1 on v0

--- a/solution.py
+++ b/solution.py
@@ -11,6 +11,8 @@
 KEY = 256
 VAL = 512
 SPAN = 128
+SKEW = 3
+PIECE = 256
 SCALE = KEY ** (-0.5)
 VMEM_BYTES = 48 * 1024 * 1024
 MESH = pl.DeviceIdType.MESH
@@ -149,8 +151,8 @@
     left = jnp.maximum(me - 1, 0)
 
     def slot(s, carry):
-        up = s - me
-        down = s - (n - 1 - me)
+        up = s - SKEW * me
+        down = s - SKEW * (n - 1 - me)
 
         @pl.when((up >= 0) & (up < pieces))
         def _():
@@ -162,7 +164,7 @@
 
         return carry
 
-    lax.fori_loop(0, pieces + n - 1, slot, 0)
+    lax.fori_loop(0, pieces + SKEW * (n - 1), slot, 0)
 
     def finish(c, carry):
         @pl.when(has_right)
@@ -178,8 +180,9 @@
     lax.fori_loop(0, pieces, finish, 0)
 
 
-def outputs_kernel(lens, q, k, v, gates, grad, fwd, bwd, *rest):
-    q_o, k_o, v_o, attn_o, scores_s, mixing_s, grown_s, cum_s = rest[-8:]
+def outputs_kernel(
+    lens, q, k, v, gates, grad, fwd, bwd, q_o, k_o, v_o, attn_o, scores_s, mixing_s, grown_s, cum_s
+):
     tokens = q.shape[0]
     blocks = tokens // SPAN
     bounds = bounds_of(lens)
@@ -211,7 +214,9 @@
         state_p = split(state)
         alive = split(grown * living)
         out = product(split(scores), value, NN) + product(alive, state_p, NT)
-        attn_o[at, :] = out.astype(BF16).astype(F32)
+        out = out.astype(BF16).astype(F32)
+        for p in range(VAL // PIECE):
+            attn_o[p, at, :] = out[:, p * PIECE : (p + 1) * PIECE]
         dq = product(split(mixing), shrunk_p, NN) + living * product(grad_p, state_p, NN)
         q_o[at, :] = (growth * dq * SCALE).astype(BF16)
         if n < blocks - 1:
@@ -242,13 +247,88 @@
             state = decay * state + product(grad_p, split(grown * living), TN)
 
 
-def weight_kernel(peers, norm, *refs):
-    out = refs[-1]
-    total = None
-    for p in range(peers):
-        term = dot(refs[p][...].astype(BF16), refs[peers + p][0].astype(BF16), TN)
-        total = term if total is None else total + term
-    out[...] = (total * norm)[None]
+def weight_kernel(n, peers, norm, *refs):
+    attn, cots, out = refs[0], refs[1 : 1 + peers], refs[1 + peers]
+    attn_in, part, ring_in, attn_send, attn_recv, ring_send, ring_recv = refs[2 + peers :]
+    pieces = attn.shape[0]
+    half = PIECE // 2
+    me, dp = lax.axis_index("ctx"), lax.axis_index("dp")
+    right, left = lax.rem(me + 1, n), lax.rem(me + n - 1, n)
+    others = [lax.rem(dp + s, peers) for s in range(1, peers)]
+
+    barrier = pltpu.get_barrier_semaphore()
+    for other in others:
+        pl.semaphore_signal(barrier, inc=1, device_id={"dp": other}, device_id_type=MESH)
+    for near in (left, right):
+        pl.semaphore_signal(barrier, inc=1, device_id={"ctx": near}, device_id_type=MESH)
+    pl.semaphore_wait(barrier, len(others) + 2)
+
+    def attn_copy(p, j):
+        return pltpu.make_async_remote_copy(
+            src_ref=attn.at[j],
+            dst_ref=attn_in.at[p, j],
+            send_sem=attn_send.at[p, j],
+            recv_sem=attn_recv.at[p, j],
+            device_id={"dp": others[p]},
+            device_id_type=MESH,
+        )
+
+    def chunk_at(way, step):
+        if way == 0:
+            return lax.rem(me - 1 - step + 2 * n, n)
+        return lax.rem(me + 1 + step, n)
+
+    def ring_copy(j, way, step):
+        return pltpu.make_async_remote_copy(
+            src_ref=part.at[j, chunk_at(way, step), pl.ds(way * half, half)],
+            dst_ref=ring_in.at[j, way, step],
+            send_sem=ring_send.at[j, way, step],
+            recv_sem=ring_recv.at[j, way, step],
+            device_id={"ctx": right if way == 0 else left},
+            device_id_type=MESH,
+        )
+
+    for j in range(pieces):
+        for p in range(peers - 1):
+            attn_copy(p, j).start()
+
+    def multiply(j):
+        for p in range(peers - 1):
+            attn_copy(p, j).wait_recv()
+        rows = [attn[j].astype(BF16)] + [attn_in[p, j].astype(BF16) for p in range(peers - 1)]
+        for c in range(n):
+            total = dot(rows[0], cots[0][c], TN)
+            for p in range(1, peers):
+                total = total + dot(rows[p], cots[p][c].astype(BF16), TN)
+            part[j, c] = total
+        for way in range(2):
+            ring_copy(j, way, 0).start()
+
+    def pass_on(j, step):
+        for way in range(2):
+            ring_copy(j, way, step - 1).wait_recv()
+            c = chunk_at(way, step)
+            rows = pl.ds(way * half, half)
+            total = part[j, c, rows, :] + ring_in[j, way, step - 1]
+            if step < n - 1:
+                part[j, c, rows, :] = total
+                ring_copy(j, way, step).start()
+            else:
+                out[pl.ds(j * PIECE + way * half, half), :] = total * norm
+
+    for t in range(pieces + n - 1):
+        if t < pieces:
+            multiply(t)
+        for j in range(pieces):
+            if 1 <= t - j <= n - 1:
+                pass_on(j, t - j)
+
+    for j in range(pieces):
+        for p in range(peers - 1):
+            attn_copy(p, j).wait_send()
+        for way in range(2):
+            for step in range(n - 1):
+                ring_copy(j, way, step).wait_send()
 
 
 def params(**more):
@@ -325,65 +405,61 @@
         name="chain",
     )(fwd, bwd, decay)
 
-    grads = []
-    attn = []
-    for h in range(heads):
-        def cols(c, h=h):
-            return pl.BlockSpec((tokens, c), lambda i: (0, h))
-
-        def state_rows(h=h):
-            return pl.BlockSpec((VAL, KEY), lambda i: (h, 0))
-
-        results = pl.pallas_call(
-            outputs_kernel,
-            grid=(1,),
-            in_specs=[smem, cols(KEY), cols(KEY), cols(VAL), cols(KEY), cols(VAL)]
-            + [state_rows()] * 2
-            + [pl.BlockSpec(memory_space=pl.ANY)] * len(grads),
-            out_specs=[
-                cols(KEY),
-                cols(KEY),
-                cols(VAL),
-                pl.BlockSpec((tokens, VAL), lambda i: (0, 0)),
-            ],
-            out_shape=[
-                jax.ShapeDtypeStruct((tokens, heads * KEY), BF16),
-                jax.ShapeDtypeStruct((tokens, heads * KEY), BF16),
-                jax.ShapeDtypeStruct((tokens, heads * VAL), BF16),
-                jax.ShapeDtypeStruct((tokens, VAL), F32),
-            ],
-            scratch_shapes=[
-                pltpu.VMEM((tokens, SPAN), F32),
-                pltpu.VMEM((tokens, SPAN), F32),
-                pltpu.VMEM((tokens, KEY), F32),
-                pltpu.VMEM((tokens, KEY), F32),
-            ],
-            input_output_aliases={8 + i: i for i in range(len(grads))},
-            compiler_params=params(),
-            cost_estimate=pl.CostEstimate(flops=3 * 10**9, bytes_accessed=8 << 20, transcendentals=0),
-            name="outputs",
-        )(doc_lengths, q, k, v, gates, grad, fwd_in, bwd_in, *grads)
-        grads = list(results[:3])
-        attn.append(results[3])
+    def state_rows():
+        return pl.BlockSpec((VAL, KEY), lambda h: (h, 0))
+
+    per_head = VAL // PIECE
+    query_grad, key_grad, value_grad, attn = pl.pallas_call(
+        outputs_kernel,
+        grid=(heads,),
+        in_specs=[smem]
+        + [head_block(tokens, c) for c in (KEY, KEY, VAL, KEY, VAL)]
+        + [state_rows()] * 2,
+        out_specs=[
+            head_block(tokens, KEY),
+            head_block(tokens, KEY),
+            head_block(tokens, VAL),
+            pl.BlockSpec((per_head, tokens, PIECE), lambda h: (h, 0, 0)),
+        ],
+        out_shape=[
+            jax.ShapeDtypeStruct((tokens, heads * KEY), BF16),
+            jax.ShapeDtypeStruct((tokens, heads * KEY), BF16),
+            jax.ShapeDtypeStruct((tokens, heads * VAL), BF16),
+            jax.ShapeDtypeStruct((heads * per_head, tokens, PIECE), F32),
+        ],
+        scratch_shapes=[
+            pltpu.VMEM((tokens, SPAN), F32),
+            pltpu.VMEM((tokens, SPAN), F32),
+            pltpu.VMEM((tokens, KEY), F32),
+            pltpu.VMEM((tokens, KEY), F32),
+        ],
+        compiler_params=params(),
+        cost_estimate=pl.CostEstimate(flops=6 * 10**9, bytes_accessed=16 << 20, transcendentals=0),
+        name="outputs",
+    )(doc_lengths, q, k, v, gates, grad, fwd_in, bwd_in)
 
     norm = 1.0 / math.sqrt(peers * n * tokens)
-    sums = []
-    for h in range(heads):
-        everyone = [attn[h]] + [shift(attn[h], s) for s in range(1, peers)]
-        partial = pl.pallas_call(
-            functools.partial(weight_kernel, peers, norm),
-            grid=(n,),
-            in_specs=[pl.BlockSpec((tokens, VAL), lambda c: (0, 0))] * peers
-            + [pl.BlockSpec((1, tokens, columns), lambda c: (c, 0, 0))] * peers,
-            out_specs=pl.BlockSpec((1, VAL, columns), lambda c: (c, 0, 0)),
-            out_shape=jax.ShapeDtypeStruct((n, VAL, columns), F32),
-            compiler_params=params(),
-            cost_estimate=pl.CostEstimate(flops=2 * 10**9, bytes_accessed=8 << 20, transcendentals=0),
-            name="weight",
-        )(*everyone, *cots)
-        sums.append(lax.psum_scatter(partial, "ctx", scatter_dimension=0, tiled=True)[0])
-    weight_grad = jnp.concatenate(sums, axis=0)
-    return (grads[0][None], grads[1][None], grads[2][None], weight_grad)
+    parts = heads * per_head
+    dma = pltpu.SemaphoreType.DMA
+    weight_grad = pl.pallas_call(
+        functools.partial(weight_kernel, n, peers, norm),
+        in_specs=[vmem] * (1 + peers),
+        out_specs=vmem,
+        out_shape=jax.ShapeDtypeStruct((heads * VAL, columns), F32),
+        scratch_shapes=[
+            pltpu.VMEM((peers - 1, parts, tokens, PIECE), F32),
+            pltpu.VMEM((parts, n, PIECE, columns), F32),
+            pltpu.VMEM((parts, 2, n - 1, PIECE // 2, columns), F32),
+            dma((peers - 1, parts)),
+            dma((peers - 1, parts)),
+            dma((parts, 2, n - 1)),
+            dma((parts, 2, n - 1)),
+        ],
+        compiler_params=params(collective_id=1, has_side_effects=True),
+        cost_estimate=pl.CostEstimate(flops=4 * 10**9, bytes_accessed=64 << 20, transcendentals=0),
+        name="weight",
+    )(attn, *cots)
+    return (query_grad[None], key_grad[None], value_grad[None], weight_grad)
 
 
 def solution(mesh):

time: 220 us -> 163 us (0.74)
  waiting for transfers between devices: 98.3 us -> 0.01 us
  Pallas kernels: 94.1 us -> 148 us
  between operations: 14.1 us -> 0.77 us
  local copies, waits for them, and re-layouts: 6.06 us -> 9.65 us
  other arithmetic: 3.73 us -> 1.51 us
    pallas_call x4 -> x2, Pallas kernels: 27.7 us -> 107 us  [the longest x1 91 us: per_device(): pl.pallas_call(functools.partial(weight_kernel, n, peers, norm), in_specs...]
    reduce_scatter x2 -> x0, waiting for transfers between devices: 67.4 us -> none  [per_device(): lax.psum_scatter(partial, 'ctx', scatter_dimension=0, tiled=True)[0]]
    ppermute x3 -> x1, waiting for transfers between devices: 30.9 us -> 0.01 us  [shift(): return lax.ppermute(x, 'dp', [(i, (i + s) % peers) for i in range(peers)])]
    pallas_call x1, Pallas kernels: 58.8 us -> 33.6 us  [per_device(): pl.pallas_call(functools.partial(chain_kernel, n, pieces), in_specs=[vmem...]
    unnamed x12 -> x15, local copies, waits for them, and re-layouts: 3.41 us -> 7 us
    concatenate x1 -> x0, other arithmetic: 2.24 us -> none  [per_device(): weight_grad = jnp.concatenate(sums, axis=0)]
  transfers between devices with their start and end apart: 5 -> 1, of which waited for: 4 -> 0; matrix products, arithmetic and copies ran while one was open for 1% -> 1% of each run, Pallas kernels for 40% -> 35%
where the time goes in v1:
time: 163 us
  Pallas kernels  148 us (91%)
  local copies, waits for them, and re-layouts  9.65 us (6%)
  starting transfers between devices  2.94 us (2%)
    pallas_call x1, Pallas kernels, per_device(): pl.pallas_call(functools.partial(weight_kernel, n, peers, norm), in_specs...  91 us
    pallas_call x1, Pallas kernels, per_device(): pl.pallas_call(functools.partial(chain_kernel, n, pieces), in_specs=[vmem...  33.6 us
    pallas_call x1, Pallas kernels, per_device(): pl.pallas_call(outputs_kernel, grid=(heads,), in_specs=[smem] + [head_blo...  15.9 us
    pallas_call x1, Pallas kernels, per_device(): pl.pallas_call(states_kernel, grid=(heads,), in_specs=[smem, head_block(t...  7.64 us
    unnamed x15, local copies, waits for them, and re-layouts  7 us
  transfers between devices with their start and end apart: 1, of which 0 were waited for; matrix products, arithmetic and copies ran while one was open for 1% of the time, Pallas kernels for 35%

profile of v1, /device:TPU:0, one launch (start us, length us, event | category | flops | bytes accessed | tf_op | source)
XLA Modules:
  0.0 163.0 jit_solution(17840457498796142318)
XLA Ops:
  0.6 2.9 %copy.11 = bf16[1,512,2048]{1,2,0:T(8,128)(2,1)S(1)} copy(bf16[1,512,2048]{2,1,0:T(8,128)(2,1)} %param.12) | data formatting | bytes 4194304 | tf_op args[5]
  3.5 1.2 constant_dynamic-slice_fusion
  4.7 0.5 copy.14
  5.2 0.0 copy-start
  5.2 0.0 copy-start.1
  5.2 0.0 copy-start.2
  5.3 0.0 copy-start.4
  5.3 1.5 convert_bitcast_fusion
  6.8 2.9 %collective-permute-start = (f32[4,512,256]{2,1,0:T(8,128)}, f32[4,512,256]{2,1,0:T(8,128)}, u32[]{:S(2)}, u32[]{:S(2)}) collective-permute-start(f32[4,512,256]{2,1,0:T(8,128)} %convert_bitcast_fusion), channel_id=1, source_target_pairs={{0,2},{2,0},{1,3},{3,1},{4,6},{6,4},{5,7},{7,5},{8,10},{10,8},{9,1... | collective-permute-start | bytes 6291464 | tf_op jit(solution)/shard_map/ppermute | solution.py:353
  9.7 1.5 copy.12
  11.2 0.0 copy-done
  11.2 0.0 copy-done.1
  11.2 0.0 copy-done.2
  11.2 0.0 copy-done.4
  11.2 0.0 copy-start.3
  11.2 1.0 copy-done.3
  12.3 7.6 %states.1 = (f32[512,1024]{1,0:T(8,128)}, f32[1024,256]{1,0:T(8,128)S(1)}, f32[1024,256]{1,0:T(8,128)S(1)}, f32[2,1,256]{2,1,0:T(1,128)S(1)}) custom-call(s32[1,6]{1,0:T(1,128)S(1)} %copy-done.4, bf16[512,512]{1,0:T(8,128)(2,1)S(1)} %bitcast.20, bf16[512,512]{1,0:T(8,128)(2,1)S(1)} %bitcast.22, bf16[512,1024]{1,0:T(8,128)(2,1)S(1)} %bitcast.18, ...), custom_call_target="tpu_custom_call" | custom-call | flops 6000000000 | bytes 14680064 | tf_op jit(solution)/shard_map/states/pallas_call | solution.py:365
  19.9 33.6 %chain.1 = (f32[1024,256]{1,0:T(8,128)S(1)}, f32[1024,256]{1,0:T(8,128)S(1)}) custom-call(f32[1024,256]{1,0:T(8,128)S(1)} %get-tuple-element.15.fwd, f32[1024,256]{1,0:T(8,128)S(1)} %get-tuple-element.16.bwd, f32[2,1,256]{2,1,0:T(1,128)S(1)} %get-tuple-element.17.decay), custom_call_target="tpu_custom_call" | custom-call | flops 1000000 | bytes 67108864 | tf_op jit(solution)/shard_map/chain/pallas_call | solution.py:397
  53.5 15.9 %outputs.1 = (bf16[512,512]{1,0:T(8,128)(2,1)}, bf16[512,512]{1,0:T(8,128)(2,1)}, bf16[512,1024]{1,0:T(8,128)(2,1)}, f32[4,512,256]{2,1,0:T(8,128)}) custom-call(s32[1,6]{1,0:T(1,128)S(1)} %copy-done.4, bf16[512,512]{1,0:T(8,128)(2,1)S(1)} %bitcast.21, bf16[512,512]{1,0:T(8,128)(2,1)S(1)} %bitcast.23, bf16[512,1024]{1,0:T(8,128)(2,1)S(1)} %bitcast.19, ...), custom_call_target="tpu_custom_call" | custom-call | flops 6000000000 | bytes 16777216 | tf_op jit(solution)/shard_map/outputs/pallas_call | solution.py:412
  69.4 0.0 collective-permute-done.refs_2_
  69.4 0.0 copy-start.5
  69.4 1.6 copy-done.5
  71.0 91.0 %weight.3 = f32[1024,256]{1,0:T(8,128)S(1)} custom-call(f32[4,512,256]{2,1,0:T(8,128)S(1)} %copy-done.5, bf16[4,512,256]{2,1,0:T(8,128)(2,1)S(1)} %bitcast.17, f32[4,512,256]{2,1,0:T(8,128)} %collective-permute-done.refs_2_), custom_call_target="tpu_custom_call" | custom-call | flops 4000000000 | bytes 67108864 | tf_op jit(solution)/shard_map/weight/pallas_call | solution.py:444
  162.1 1.0 copy.16
Async XLA Ops:
  5.2 6.0 %copy-start = (bf16[1,512,1024]{2,1,0:T(8,128)(2,1)S(1)}, bf16[1,512,1024]{2,1,0:T(8,128)(2,1)}, u32[]{:S(2)}) copy-start(bf16[1,512,1024]{2,1,0:T(8,128)(2,1)} %param.9) | copy-start | bytes 3145732
  5.2 6.0 %copy-start.1 = (bf16[1,512,512]{2,1,0:T(8,128)(2,1)S(1)}, bf16[1,512,512]{2,1,0:T(8,128)(2,1)}, u32[]{:S(2)}) copy-start(bf16[1,512,512]{2,1,0:T(8,128)(2,1)} %param.7) | copy-start | bytes 1572868
  5.2 6.0 %copy-start.2 = (bf16[1,512,512]{2,1,0:T(8,128)(2,1)S(1)}, bf16[1,512,512]{2,1,0:T(8,128)(2,1)}, u32[]{:S(2)}) copy-start(bf16[1,512,512]{2,1,0:T(8,128)(2,1)} %param.8) | copy-start | bytes 1572868
  5.3 6.0 %copy-start.4 = (s32[1,6]{1,0:T(1,128)S(1)}, s32[1,6]{1,0:T(1,128)}, u32[]{:S(2)}) copy-start(s32[1,6]{1,0:T(1,128)} %lens.3) | copy-start | bytes 76
  6.8 62.7 %collective-permute-start = (f32[4,512,256]{2,1,0:T(8,128)}, f32[4,512,256]{2,1,0:T(8,128)}, u32[]{:S(2)}, u32[]{:S(2)}) collective-permute-start(f32[4,512,256]{2,1,0:T(8,128)} %convert_bitcast_fusion), channel_id=1, source_target_pairs={{0,2},{2,0},{1,3},{3,1},{4,6},{6,4},{5,7},{7,5},{8,10},{10,8},{9,1... | collective-permute-start | bytes 6291464 | tf_op jit(solution)/shard_map/ppermute | solution.py:353
  11.2 1.0 copy-start.3
  69.4 1.6 copy-start.5

commit v2 on v1

v2 whole, which is shorter than its diff:
```python
import functools
import math

import jax
import jax.numpy as jnp
from jax import lax
from jax.experimental import pallas as pl
from jax.experimental.pallas import tpu as pltpu
from jax.sharding import PartitionSpec as P

KEY = 256
VAL = 512
SPAN = 128
SKEW = 3
PIECE = 256
SCALE = KEY ** (-0.5)
VMEM_BYTES = 60 * 1024 * 1024
MESH = pl.DeviceIdType.MESH
F32 = jnp.float32
BF16 = jnp.bfloat16

NN = (((1,), (0,)), ((), ()))
NT = (((1,), (1,)), ((), ()))
TN = (((0,), (0,)), ((), ()))


def dot(a, b, dims):
    return lax.dot_general(a, b, dims, preferred_element_type=F32)


def split(x):
    high = x.astype(BF16)
    return high, (x - high.astype(F32)).astype(BF16)


def whole(x):
    return x, None


def product(a, b, dims):
    out = dot(a[0], b[0], dims)
    if a[1] is not None:
        out = out + dot(a[1], b[0], dims)
    if b[1] is not None:
        out = out + dot(a[0], b[1], dims)
    return out


def bounds_of(lens_ref):
    bounds, total = [], 0
    for d in range(lens_ref.shape[1]):
        total = total + lens_ref[0, d]
        bounds.append(total)
    return bounds


def doc_scalar(bounds, position):
    count = jnp.int32(0)
    for bound in bounds:
        count = count + jnp.where(position >= bound, 1, 0).astype(jnp.int32)
    return count


def doc_array(bounds, first, shape, dim):
    positions = first + lax.broadcasted_iota(jnp.int32, shape, dim)
    count = jnp.zeros(shape, jnp.int32)
    for bound in bounds:
        count = count + jnp.where(positions >= bound, 1, 0)
    return count


def alive_and_trailing(bounds, first, rows, columns):
    docs = doc_array(bounds, first, (rows, columns), 0)
    before = jnp.where(first > 0, doc_scalar(bounds, first - 1), -1)
    last = doc_scalar(bounds, first + rows - 1)
    living = jnp.where(docs == before, 1.0, 0.0).astype(F32)
    trailing = jnp.where(docs == last, 1.0, 0.0).astype(F32)
    return living, trailing


def running_sum(gates):
    rows = gates.shape[0]
    lower = lax.broadcasted_iota(jnp.int32, (rows, rows), 0) >= lax.broadcasted_iota(
        jnp.int32, (rows, rows), 1
    )
    return dot(jnp.where(lower, 1.0, 0.0).astype(BF16), gates, NN)


def states_kernel(n, peers, lens, q, k, v, gates, cot, weight, *outs):
    grad_o, fwd_o, bwd_o, decay_o = outs[:4]
    tokens = q.shape[0]
    if len(outs) > 4:
        cot_own, cot_send = outs[4:]
        dp = lax.axis_index("dp")
        columns = cot.shape[1] // (n * peers)

        @pl.when(pl.program_id(0) == 0)
        def _():
            for c in range(n):
                to = slice(c * columns, (c + 1) * columns)
                for s in range(peers):
                    start = (c * peers + lax.rem(dp + s, peers)) * columns
                    part = cot[:, pl.ds(pl.multiple_of(start, columns), columns)]
                    if s == 0:
                        cot_own[:, to] = part
                    else:
                        cot_send[s - 1, :, to] = part.astype(F32)

    bounds = bounds_of(lens)
    first = lax.axis_index("ctx") * tokens
    grad = dot(cot[...], weight[...], NT)
    grad_o[...] = grad
    cumulative = running_sum(gates[...])
    end = cumulative[tokens - 1 :, :]
    living, trailing = alive_and_trailing(bounds, first, tokens, KEY)
    tail = k[...].astype(F32) * jnp.exp(end - cumulative) * trailing
    alive = q[...].astype(F32) * SCALE * jnp.exp(cumulative) * living
    fwd_o[...] = product(whole(v[...]), split(tail), TN)
    bwd_o[...] = product(split(grad), split(alive), TN)
    decay_o[...] = (jnp.exp(end) * living[tokens - 1 :, :])[None]


def main_kernel(
    n, peers, pieces, norm,
    lens, q, k, v, gates, grad, fwd, bwd, decay, cot_own, cot_send,
    q_o, k_o, v_o, out,
    f_send, b_send, f_recv, b_recv, cum_s, attn_l, dq_l, dk_l, dv_l, fwd_c, bwd_c,
    cot_in, attn, attn_in, part, ring_in,
    chain_sems, cot_sems, attn_send, attn_recv, ring_send, ring_recv,
):
    me, dp, mp = lax.axis_index("ctx"), lax.axis_index("dp"), lax.axis_index("mp")
    tokens = q.shape[0]
    heads = decay.shape[0]
    blocks = tokens // SPAN
    cores = lax.axis_size("mp")
    right, left = lax.rem(me + 1, n), lax.rem(me + n - 1, n)
    others = [lax.rem(dp + s, peers) for s in range(1, peers)]
    mates = [lax.rem(mp + s, cores) for s in range(1, cores)]

    barrier = pltpu.get_barrier_semaphore()
    for other in others:
        pl.semaphore_signal(barrier, inc=1, device_id={"dp": other}, device_id_type=MESH)
    for near in (left, right):
        pl.semaphore_signal(barrier, inc=1, device_id={"ctx": near}, device_id_type=MESH)
    for mate in mates:
        pl.semaphore_signal(barrier, inc=1, device_id={"mp": mate}, device_id_type=MESH)
    pl.semaphore_wait(barrier, len(others) + 2 + len(mates))

    share = tokens // cores

    def remote(src, dst, send_sem, recv_sem, to):
        return pltpu.make_async_remote_copy(
            src_ref=src, dst_ref=dst, send_sem=send_sem, recv_sem=recv_sem,
            device_id=to, device_id_type=MESH,
        )

    def cot_copy(p):
        rows = pl.ds(pl.multiple_of(mp * share, share), share)
        return remote(
            cot_send.at[p, rows], cot_in.at[p, rows], cot_sems.at[0, p, 0], cot_sems.at[1, p, 0],
            {"dp": others[p]},
        )

    def mate_copy(p, m):
        rows = pl.ds(pl.multiple_of(mp * share, share), share)
        return remote(
            cot_in.at[p, rows], cot_in.at[p, rows], cot_sems.at[0, p, m + 1],
            cot_sems.at[1, p, m + 1], {"mp": mates[m]},
        )

    for p in range(peers - 1):
        cot_copy(p).start()

    rows_each = fwd.shape[0] // pieces
    per_head = pieces // heads
    has_left, has_right = me > 0, me < n - 1

    def chain_copy(c, send, recv, base, to):
        at = pl.ds(pl.multiple_of(c * rows_each, rows_each), rows_each)
        return remote(
            send.at[at], recv.at[at], chain_sems.at[base, c], chain_sems.at[base + 1, c], {"ctx": to}
        )

    def chain_piece(c, own, send, recv, base, has_source, has_target, to):
        at = pl.ds(pl.multiple_of(c * rows_each, rows_each), rows_each)

        @pl.when(has_source)
        def _():
            chain_copy(c, send, recv, base, to).wait_recv()

        @pl.when(jnp.logical_not(has_source))
        def _():
            recv[at, :] = jnp.zeros((rows_each, KEY), F32)

        @pl.when(has_target)
        def _():
            send[at, :] = decay[c // per_head] * recv[at, :] + own[at, :]
            chain_copy(c, send, recv, base, to).start()

    def slot(s, carry):
        up = s - SKEW * me
        down = s - SKEW * (n - 1 - me)

        @pl.when((up >= 0) & (up < pieces))
        def _():
            chain_piece(up, fwd, f_send, f_recv, 0, has_left, has_right, right)

        @pl.when((down >= 0) & (down < pieces))
        def _():
            chain_piece(down, bwd, b_send, b_recv, 2, has_right, has_left, left)

        return carry

    bounds = bounds_of(lens)
    device_first = me * tokens

    def of_head(h, n_block):
        at = slice(n_block * SPAN, (n_block + 1) * SPAN)
        return at, slice(h * KEY, (h + 1) * KEY), slice(h * VAL, (h + 1) * VAL)

    def inner(h, n_block):
        at, hk, hv = of_head(h, n_block)
        first = device_first + n_block * SPAN
        cumulative = running_sum(gates[at, hk])
        cum_s[at, hk] = cumulative
        growth = jnp.exp(cumulative)
        shrink = jnp.exp(-cumulative)
        end = cumulative[SPAN - 1 :, :]
        living, trailing = alive_and_trailing(bounds, first, SPAN, KEY)
        rows = lax.broadcasted_iota(jnp.int32, (SPAN, SPAN), 0)
        columns = lax.broadcasted_iota(jnp.int32, (SPAN, SPAN), 1)
        same = doc_array(bounds, first, (SPAN, SPAN), 0) == doc_array(bounds, first, (SPAN, SPAN), 1)
        mask = jnp.where((rows >= columns) & same, 1.0, 0.0).astype(F32)
        value = whole(v[at, hv])
        key = k[at, hk].astype(F32)
        grown = q[at, hk].astype(F32) * SCALE * growth
        grown_p, shrunk_p, grad_p = split(grown), split(key * shrink), split(grad[at, hv])
        scores = split(product(grown_p, shrunk_p, NT) * mask)
        mixing = split(product(grad_p, value, NT) * mask)
        attn_l[at, hv] = product(scores, value, NN)
        dq_l[at, hk] = product(mixing, shrunk_p, NN)
        dk_l[at, hk] = shrink * product(mixing, grown_p, TN)
        dv_l[at, hv] = product(scores, grad_p, TN)
        if n_block < blocks - 1:
            tail = split(key * jnp.exp(end - cumulative) * trailing)
            fwd_c[h, n_block] = product(value, tail, TN)
        if n_block > 0:
            bwd_c[h, n_block - 1] = product(grad_p, split(grown * living), TN)

    units = [(h, b) for h in range(heads) for b in range(blocks)]
    slots = pieces + SKEW * (n - 1)
    done = 0
    for u, (h, b) in enumerate(units):
        until = (u + 1) * slots // len(units)
        lax.fori_loop(done, until, slot, 0)
        done = until
        inner(h, b)

    for p in range(peers - 1):
        cot_copy(p).wait_recv()
        for m in range(cores - 1):
            mate_copy(p, m).start()

    def attn_copy(p, j):
        return remote(
            attn.at[j], attn_in.at[p, j], attn_send.at[p, j], attn_recv.at[p, j], {"dp": others[p]}
        )

    parts_of_head = VAL // PIECE

    def forward(h):
        state = f_recv[h * VAL : (h + 1) * VAL, :]
        for b in range(blocks):
            at, hk, hv = of_head(h, b)
            cumulative = cum_s[at, hk]
            growth = jnp.exp(cumulative)
            living, _ = alive_and_trailing(bounds, device_first + b * SPAN, SPAN, KEY)
            alive = split(q[at, hk].astype(F32) * SCALE * growth * living)
            state_p = split(state)
            total = attn_l[at, hv] + product(alive, state_p, NT)
            total = total.astype(BF16).astype(F32)
            for p in range(parts_of_head):
                attn[h * parts_of_head + p, at, :] = total[:, p * PIECE : (p + 1) * PIECE]
            dq = dq_l[at, hk] + living * product(split(grad[at, hv]), state_p, NN)
            q_o[at, hk] = (growth * dq * SCALE).astype(BF16)
            if b < blocks - 1:
                keep = growth[SPAN - 1 :, :] * living[SPAN - 1 :, :]
                state = keep * state + fwd_c[h, b]

    def backward(h):
        state = b_recv[h * VAL : (h + 1) * VAL, :]
        for b in reversed(range(blocks)):
            at, hk, hv = of_head(h, b)
            cumulative = cum_s[at, hk]
            end = cumulative[SPAN - 1 :, :]
            living, trailing = alive_and_trailing(bounds, device_first + b * SPAN, SPAN, KEY)
            from_end = jnp.exp(end - cumulative) * trailing
            tail = split(k[at, hk].astype(F32) * from_end)
            state_p = split(state)
            dk = dk_l[at, hk] + from_end * product(whole(v[at, hv]), state_p, NN)
            k_o[at, hk] = dk.astype(BF16)
            v_o[at, hv] = (dv_l[at, hv] + product(tail, state_p, NT)).astype(BF16)
            if b > 0:
                keep = jnp.exp(end) * living[SPAN - 1 :, :]
                state = keep * state + bwd_c[h, b - 1]

    for h in range(heads):
        forward(h)
        for j in range(h * parts_of_head, (h + 1) * parts_of_head):
            for p in range(peers - 1):
                attn_copy(p, j).start()
    for h in range(heads):
        backward(h)

    half = PIECE // 2
    columns = out.shape[1]
    parts = attn.shape[0]

    def chunk_at(way, step):
        if way == 0:
            return lax.rem(me - 1 - step + 2 * n, n)
        return lax.rem(me + 1 + step, n)

    def ring_copy(j, way, step):
        return remote(
            part.at[j, chunk_at(way, step), pl.ds(way * half, half)],
            ring_in.at[j, way, step],
            ring_send.at[j, way, step],
            ring_recv.at[j, way, step],
            {"ctx": right if way == 0 else left},
        )

    for p in range(peers - 1):
        for m in range(cores - 1):
            mate_copy(p, m).wait_recv()

    def multiply(j):
        total = dot(attn[j].astype(BF16), cot_own[...], TN)
        for p in range(peers - 1):
            attn_copy(p, j).wait_recv()
            total = total + dot(attn_in[p, j].astype(BF16), cot_in[p].astype(BF16), TN)
        for c in range(n):
            part[j, c] = total[:, c * columns : (c + 1) * columns]
        for way in range(2):
            ring_copy(j, way, 0).start()

    def pass_on(j, step):
        for way in range(2):
            ring_copy(j, way, step - 1).wait_recv()
            c = chunk_at(way, step)
            rows = pl.ds(way * half, half)
            total = part[j, c, rows, :] + ring_in[j, way, step - 1]
            if step < n - 1:
                part[j, c, rows, :] = total
                ring_copy(j, way, step).start()
            else:
                out[pl.ds(j * PIECE + way * half, half), :] = total * norm

    for t in range(parts + n - 1):
        if t < parts:
            multiply(t)
        for j in range(parts):
            if 1 <= t - j <= n - 1:
                pass_on(j, t - j)

    def finish(c, carry):
        @pl.when(has_right)
        def _():
            chain_copy(c, f_send, f_recv, 0, right).wait_send()

        @pl.when(has_left)
        def _():
            chain_copy(c, b_send, b_recv, 2, left).wait_send()

        return carry

    lax.fori_loop(0, pieces, finish, 0)
    for p in range(peers - 1):
        cot_copy(p).wait_send()
        for m in range(cores - 1):
            mate_copy(p, m).wait_send()
    for j in range(parts):
        for p in range(peers - 1):
            attn_copy(p, j).wait_send()
        for way in range(2):
            for step in range(n - 1):
                ring_copy(j, way, step).wait_send()


def params(**more):
    return pltpu.CompilerParams(vmem_limit_bytes=VMEM_BYTES, **more)


def per_device(queries, key_vectors, value_vectors, log_gates, doc_lengths, cotangent, out_weight):
    q, k, v, gates, cot = (x[0] for x in (queries, key_vectors, value_vectors, log_gates, cotangent))
    tokens, width = cot.shape
    heads = out_weight.shape[0] // VAL
    n, peers = lax.axis_size("ctx"), lax.axis_size("dp")
    dp = lax.axis_index("dp")
    columns = width // (n * peers)
    smem = pl.BlockSpec(memory_space=pltpu.SMEM)

    in_kernel = columns % 128 == 0
    spread = n * columns

    def head_block(rows, cols):
        return pl.BlockSpec((rows, cols), lambda h: (0, h))

    def head_rows(rows, cols):
        return pl.BlockSpec((rows, cols), lambda h: (h, 0))

    grad, fwd, bwd, decay, *cots = pl.pallas_call(
        functools.partial(states_kernel, n, peers),
        grid=(heads,),
        in_specs=[
            smem,
            head_block(tokens, KEY),
            head_block(tokens, KEY),
            head_block(tokens, VAL),
            head_block(tokens, KEY),
            pl.BlockSpec((tokens, width), lambda h: (0, 0)),
            head_rows(VAL, width),
        ],
        out_specs=[
            head_block(tokens, VAL),
            head_rows(VAL, KEY),
            head_rows(VAL, KEY),
            pl.BlockSpec((1, 1, KEY), lambda h: (h, 0, 0)),
        ]
        + [
            pl.BlockSpec((tokens, spread), lambda h: (0, 0)),
            pl.BlockSpec((peers - 1, tokens, spread), lambda h: (0, 0, 0)),
        ]
        * in_kernel,
        out_shape=[
            jax.ShapeDtypeStruct((tokens, heads * VAL), F32),
            jax.ShapeDtypeStruct((heads * VAL, KEY), F32),
            jax.ShapeDtypeStruct((heads * VAL, KEY), F32),
            jax.ShapeDtypeStruct((heads, 1, KEY), F32),
        ]
        + [
            jax.ShapeDtypeStruct((tokens, spread), BF16),
            jax.ShapeDtypeStruct((peers - 1, tokens, spread), F32),
        ]
        * in_kernel,
        compiler_params=params(),
        cost_estimate=pl.CostEstimate(flops=6 * 10**9, bytes_accessed=14 << 20, transcendentals=0),
        name="states",
    )(doc_lengths, q, k, v, gates, cot, out_weight)

    if in_kernel:
        cot_own, cot_send = cots
    else:
        parted = cot.reshape(tokens, n, peers, columns)
        shares = [
            lax.dynamic_index_in_dim(parted, lax.rem(dp + s, peers), axis=2, keepdims=False).reshape(
                tokens, spread
            )
            for s in range(peers)
        ]
        cot_own, cot_send = shares[0], jnp.stack(shares[1:]).astype(F32)

    pieces = 8 * heads
    vmem = pl.BlockSpec(memory_space=pltpu.VMEM)
    states = (heads * VAL, KEY)
    keys, values = (tokens, heads * KEY), (tokens, heads * VAL)
    parts = heads * VAL // PIECE
    blocks = tokens // SPAN
    cores = lax.axis_size("mp")
    dma = pltpu.SemaphoreType.DMA
    norm = 1.0 / math.sqrt(peers * n * tokens)
    scratch = (
        [states] * 4
        + [keys, values, keys, keys, values]
        + [(heads, blocks - 1, VAL, KEY)] * 2
        + [
            (peers - 1, tokens, spread),
            (parts, tokens, PIECE),
            (peers - 1, parts, tokens, PIECE),
            (parts, n, PIECE, columns),
            (parts, 2, n - 1, PIECE // 2, columns),
        ]
    )
    query_grad, key_grad, value_grad, weight_grad = pl.pallas_call(
        functools.partial(main_kernel, n, peers, pieces, norm),
        in_specs=[smem] + [vmem] * 10,
        out_specs=[vmem] * 4,
        out_shape=[
            jax.ShapeDtypeStruct(keys, BF16),
            jax.ShapeDtypeStruct(keys, BF16),
            jax.ShapeDtypeStruct(values, BF16),
            jax.ShapeDtypeStruct((heads * VAL, columns), F32),
        ],
        scratch_shapes=[pltpu.VMEM(shape, F32) for shape in scratch]
        + [
            dma((4, pieces)),
            dma((2, peers - 1, cores)),
            dma((peers - 1, parts)),
            dma((peers - 1, parts)),
            dma((parts, 2, n - 1)),
            dma((parts, 2, n - 1)),
        ],
        compiler_params=params(collective_id=0, has_side_effects=True),
        cost_estimate=pl.CostEstimate(flops=10**10, bytes_accessed=64 << 20, transcendentals=0),
        name="main",
    )(doc_lengths, q, k, v, gates, grad, fwd, bwd, decay, cot_own, cot_send)
    return (query_grad[None], key_grad[None], value_grad[None], weight_grad)


def solution(mesh):
    batch = ("groups", "dp")
    return jax.shard_map(
        per_device,
        mesh=mesh,
        in_specs=(
            P(batch, "ctx", "mp"),
            P(batch, "ctx", "mp"),
            P(batch, "ctx", "mp"),
            P(batch, "ctx", "mp"),
            P(batch, None),
            P(batch, "ctx", None),
            P("mp", None),
        ),
        out_specs=(
            P(batch, "ctx", "mp"),
            P(batch, "ctx", "mp"),
            P(batch, "ctx", "mp"),
            P(("groups", "mp"), ("ctx", "dp")),
        ),
        check_vma=False,
    )
```

time: 163 us -> 151 us (0.926)
  Pallas kernels: 148 us -> 144 us
  local copies, waits for them, and re-layouts: 9.65 us -> 5.83 us
  starting transfers between devices: 2.94 us -> 0 us
    pallas_call x4 -> x2, Pallas kernels: 148 us -> 144 us  [the longest x1 134 us: per_device(): pl.pallas_call(functools.partial(main_kernel, n, peers, pieces, norm), in...]
    ppermute x1 -> x0, starting transfers between devices: 2.94 us -> none  [shift(): return lax.ppermute(x, 'dp', [(i, (i + s) % peers) for i in range(peers)])]
    dynamic_slice x2 -> x0, local copies, waits for them, and re-layouts: 2.65 us -> none  [part_for(): lax.dynamic_index_in_dim(parted, p, axis=2, keepdims=False)]
    unnamed x15 -> x8, local copies, waits for them, and re-layouts: 7 us -> 5.83 us
  transfers between devices with their start and end apart: 1 -> 0, of which waited for: 0 -> 0; matrix products, arithmetic and copies ran while one was open for 1% -> 0% of each run, Pallas kernels for 35% -> 0%
where the time goes in v2:
time: 151 us
  Pallas kernels  144 us (95%)
  local copies, waits for them, and re-layouts  5.83 us (4%)
    pallas_call x1, Pallas kernels, per_device(): pl.pallas_call(functools.partial(main_kernel, n, peers, pieces, norm), in...  134 us
    pallas_call x1, Pallas kernels, per_device(): pl.pallas_call(functools.partial(states_kernel, n, peers), grid=(heads,),...  10.4 us
    unnamed x8, local copies, waits for them, and re-layouts  5.83 us

profile of v2, /device:TPU:0, one launch (start us, length us, event | category | flops | bytes accessed | tf_op | source)
XLA Modules:
  0.0 150.8 jit_solution(4007910901882469033)
XLA Ops:
  0.6 10.4 %states.1 = (f32[512,1024]{1,0:T(8,128)}, f32[1024,256]{1,0:T(8,128)}, f32[1024,256]{1,0:T(8,128)}, f32[2,1,256]{2,1,0:T(1,128)}, bf16[512,1024]{1,0:T(8,128)(2,1)}, /*index=5*/f32[1,512,1024]{2,1,0:T(8,128)}) custom-call(s32[1,6]{1,0:T(1,128)} %lens.3, bf16[512,512]{1,0:T(8,128)(2,1)} %bitcast.14, bf16[512,512]{1,0:T(8,128)(2,1)} %bitcast.16, ...), custom_call_target="tpu_custom_call" | custom-call | flops 6000000000 | bytes 14680064 | tf_op jit(solution)/shard_map/states/pallas_call | solution.py:412
  11.1 133.8 %main.1 = (bf16[512,512]{1,0:T(8,128)(2,1)}, bf16[512,512]{1,0:T(8,128)(2,1)}, bf16[512,1024]{1,0:T(8,128)(2,1)}, f32[1024,256]{1,0:T(8,128)}) custom-call(s32[1,6]{1,0:T(1,128)} %lens.3, bf16[512,512]{1,0:T(8,128)(2,1)} %bitcast.15, bf16[512,512]{1,0:T(8,128)(2,1)} %bitcast.17, bf16[512,1024]{1,0:T(8,128)(2,1)} %bitcast.13, bf16[512,512]{1,0:T(8,128)(2,1)} %bitcast.19, ...), custom_call_target="tpu_custom_call" | custom-call | flops 10000000000 | bytes 67108864 | tf_op jit(solution)/shard_map/main/pallas_call | solution.py:484
  144.9 0.0 copy-start.1
  144.9 0.0 copy-start
  144.9 2.0 %copy.15 = bf16[1,512,512]{2,1,0:T(8,128)(2,1)} copy(bf16[1,512,512]{2,1,0:T(8,128)(2,1)} %bitcast.10) | data formatting | bytes 1048576
  147.0 1.9 %copy.16 = bf16[1,512,512]{2,1,0:T(8,128)(2,1)} copy(bf16[1,512,512]{2,1,0:T(8,128)(2,1)} %bitcast.9) | data formatting | bytes 1048576
  148.8 0.0 copy-done.1
  148.8 1.0 copy.17
  149.8 0.0 copy-done
  149.8 1.0 copy.18
Async XLA Ops:
  144.9 3.9 %copy-start.1 = (bf16[512,1024]{1,0:T(8,128)(2,1)S(1)}, bf16[512,1024]{1,0:T(8,128)(2,1)}, u32[]{:S(2)}) copy-start(bf16[512,1024]{1,0:T(8,128)(2,1)} %get-tuple-element.22) | copy-start | bytes 3145732
  144.9 4.9 %copy-start = (f32[1024,256]{1,0:T(8,128)S(1)}, f32[1024,256]{1,0:T(8,128)}, u32[]{:S(2)}) copy-start(f32[1024,256]{1,0:T(8,128)} %get-tuple-element.31) | copy-start | bytes 3145732

commit v3 on v2

--- a/solution.py
+++ b/solution.py
@@ -125,8 +125,8 @@
     lens, q, k, v, gates, grad, fwd, bwd, decay, cot_own, cot_send,
     q_o, k_o, v_o, out,
     f_send, b_send, f_recv, b_recv, cum_s, attn_l, dq_l, dk_l, dv_l, fwd_c, bwd_c,
-    cot_in, attn, attn_in, part, ring_in,
-    chain_sems, cot_sems, attn_send, attn_recv, ring_send, ring_recv,
+    cot_in, attn, attn_in, part, line_in,
+    chain_sems, cot_sems, attn_send, attn_recv, line_send, line_recv,
 ):
     me, dp, mp = lax.axis_index("ctx"), lax.axis_index("dp"), lax.axis_index("mp")
     tokens = q.shape[0]
@@ -247,20 +247,6 @@
         if n_block > 0:
             bwd_c[h, n_block - 1] = product(grad_p, split(grown * living), TN)
 
-    units = [(h, b) for h in range(heads) for b in range(blocks)]
-    slots = pieces + SKEW * (n - 1)
-    done = 0
-    for u, (h, b) in enumerate(units):
-        until = (u + 1) * slots // len(units)
-        lax.fori_loop(done, until, slot, 0)
-        done = until
-        inner(h, b)
-
-    for p in range(peers - 1):
-        cot_copy(p).wait_recv()
-        for m in range(cores - 1):
-            mate_copy(p, m).start()
-
     def attn_copy(p, j):
         return remote(
             attn.at[j], attn_in.at[p, j], attn_send.at[p, j], attn_recv.at[p, j], {"dp": others[p]}
@@ -304,30 +290,44 @@
                 keep = jnp.exp(end) * living[SPAN - 1 :, :]
                 state = keep * state + bwd_c[h, b - 1]
 
+    done, waiting = 0, [(h, b) for h in range(heads) for b in range(blocks)]
     for h in range(heads):
+        target = (h + 1) * per_head + SKEW * (n - 1)
+        own = [u for u in waiting if u[0] <= h]
+        more = [u for u in waiting if u[0] > h][: blocks // 2]
+        waiting = [u for u in waiting if u not in own and u not in more]
+        start = done
+        for i, unit in enumerate(own + more):
+            until = start + (i + 1) * (target - start) // len(own + more)
+            lax.fori_loop(done, until, slot, 0)
+            done = until
+            inner(*unit)
+        lax.fori_loop(done, target, slot, 0)
+        done = target
         forward(h)
         for j in range(h * parts_of_head, (h + 1) * parts_of_head):
             for p in range(peers - 1):
                 attn_copy(p, j).start()
-    for h in range(heads):
-        backward(h)
-
-    half = PIECE // 2
+
+    for p in range(peers - 1):
+        cot_copy(p).wait_recv()
+        for m in range(cores - 1):
+            mate_copy(p, m).start()
+
     columns = out.shape[1]
     parts = attn.shape[0]
 
-    def chunk_at(way, step):
-        if way == 0:
-            return lax.rem(me - 1 - step + 2 * n, n)
-        return lax.rem(me + 1 + step, n)
-
-    def ring_copy(j, way, step):
-        return remote(
-            part.at[j, chunk_at(way, step), pl.ds(way * half, half)],
-            ring_in.at[j, way, step],
-            ring_send.at[j, way, step],
-            ring_recv.at[j, way, step],
-            {"ctx": right if way == 0 else left},
+    def line_copy(j, c, up):
+        place = c if up else jnp.where(me - 1 == c, n, c)
+        return remote(
+            part.at[j, c], line_in.at[j, place], line_send.at[j, c], line_recv.at[j, place],
+            {"ctx": right if up else left},
+        )
+
+    def arrival(j, place, up):
+        return remote(
+            part.at[j, 0], line_in.at[j, place], line_send.at[j, 0], line_recv.at[j, place],
+            {"ctx": right if up else left},
         )
 
     for p in range(peers - 1):
@@ -341,27 +341,54 @@
             total = total + dot(attn_in[p, j].astype(BF16), cot_in[p].astype(BF16), TN)
         for c in range(n):
             part[j, c] = total[:, c * columns : (c + 1) * columns]
-        for way in range(2):
-            ring_copy(j, way, 0).start()
-
-    def pass_on(j, step):
-        for way in range(2):
-            ring_copy(j, way, step - 1).wait_recv()
-            c = chunk_at(way, step)
-            rows = pl.ds(way * half, half)
-            total = part[j, c, rows, :] + ring_in[j, way, step - 1]
-            if step < n - 1:
-                part[j, c, rows, :] = total
-                ring_copy(j, way, step).start()
-            else:
-                out[pl.ds(j * PIECE + way * half, half), :] = total * norm
-
-    for t in range(parts + n - 1):
-        if t < parts:
-            multiply(t)
-        for j in range(parts):
-            if 1 <= t - j <= n - 1:
-                pass_on(j, t - j)
+
+    def sent(j, c):
+        return remote(
+            part.at[j, c], line_in.at[j, c], line_send.at[j, c], line_recv.at[j, c], {"ctx": right}
+        )
+
+    def add_and_send(j, c, up, has_source):
+        @pl.when(has_source)
+        def _():
+            arrival(j, c, up).wait_recv()
+            part[j, c] = part[j, c] + line_in[j, c]
+
+        line_copy(j, c, up).start()
+
+    def pass_on(j):
+        for c in reversed(range(1, n)):
+
+            @pl.when(me < c)
+            def _():
+                add_and_send(j, c, True, has_left)
+
+        for c in range(n - 1):
+
+            @pl.when(me > c)
+            def _():
+                add_and_send(j, c, False, has_right)
+
+    def settle(j):
+        at = pl.ds(j * PIECE, PIECE)
+        out[at, :] = part[j, me] * norm
+
+        @pl.when(has_left)
+        def _():
+            arrival(j, me, True).wait_recv()
+            out[at, :] = out[at, :] + line_in[j, me] * norm
+
+        @pl.when(has_right)
+        def _():
+            arrival(j, n, False).wait_recv()
+            out[at, :] = out[at, :] + line_in[j, n] * norm
+
+    for j in range(parts):
+        multiply(j)
+        pass_on(j)
+        if j < heads:
+            backward(j)
+    for j in range(parts):
+        settle(j)
 
     def finish(c, carry):
         @pl.when(has_right)
@@ -382,9 +409,11 @@
     for j in range(parts):
         for p in range(peers - 1):
             attn_copy(p, j).wait_send()
-        for way in range(2):
-            for step in range(n - 1):
-                ring_copy(j, way, step).wait_send()
+        for c in range(n):
+
+            @pl.when(me != c)
+            def _():
+                sent(j, c).wait_send()
 
 
 def params(**more):
@@ -478,7 +507,7 @@
             (parts, tokens, PIECE),
             (peers - 1, parts, tokens, PIECE),
             (parts, n, PIECE, columns),
-            (parts, 2, n - 1, PIECE // 2, columns),
+            (parts, n + 1, PIECE, columns),
         ]
     )
     query_grad, key_grad, value_grad, weight_grad = pl.pallas_call(
@@ -497,8 +526,8 @@
             dma((2, peers - 1, cores)),
             dma((peers - 1, parts)),
             dma((peers - 1, parts)),
-            dma((parts, 2, n - 1)),
-            dma((parts, 2, n - 1)),
+            dma((parts, n)),
+            dma((parts, n + 1)),
         ],
         compiler_params=params(collective_id=0, has_side_effects=True),
         cost_estimate=pl.CostEstimate(flops=10**10, bytes_accessed=64 << 20, transcendentals=0),

time: 151 us -> 146 us (0.967)
  Pallas kernels: 144 us -> 139 us
    pallas_call x1, Pallas kernels: 134 us -> 128 us  [per_device(): pl.pallas_call(functools.partial(main_kernel, n, peers, pieces, norm), in...]
where the time goes in v3:
time: 146 us; the launch traced here: 145 us
  Pallas kernels  139 us (95%)
  local copies, waits for them, and re-layouts  5.83 us (4%)
    pallas_call x1, Pallas kernels, per_device(): pl.pallas_call(functools.partial(main_kernel, n, peers, pieces, norm), in...  128 us
    pallas_call x1, Pallas kernels, per_device(): pl.pallas_call(functools.partial(states_kernel, n, peers), grid=(heads,),...  10.4 us
    unnamed x8, local copies, waits for them, and re-layouts  5.83 us

profile of v3, /device:TPU:0, one launch (start us, length us, event | category | flops | bytes accessed | tf_op | source)
XLA Modules:
  0.0 145.4 jit_solution(10900895456255468027)
XLA Ops:
  0.6 10.4 %states.1 = (f32[512,1024]{1,0:T(8,128)}, f32[1024,256]{1,0:T(8,128)}, f32[1024,256]{1,0:T(8,128)}, f32[2,1,256]{2,1,0:T(1,128)}, bf16[512,1024]{1,0:T(8,128)(2,1)}, /*index=5*/f32[1,512,1024]{2,1,0:T(8,128)}) custom-call(s32[1,6]{1,0:T(1,128)} %lens.3, bf16[512,512]{1,0:T(8,128)(2,1)} %bitcast.14, bf16[512,512]{1,0:T(8,128)(2,1)} %bitcast.16, ...), custom_call_target="tpu_custom_call" | custom-call | flops 6000000000 | bytes 14680064 | tf_op jit(solution)/shard_map/states/pallas_call | solution.py:441
  11.1 128.5 %main.1 = (bf16[512,512]{1,0:T(8,128)(2,1)}, bf16[512,512]{1,0:T(8,128)(2,1)}, bf16[512,1024]{1,0:T(8,128)(2,1)}, f32[1024,256]{1,0:T(8,128)}) custom-call(s32[1,6]{1,0:T(1,128)} %lens.3, bf16[512,512]{1,0:T(8,128)(2,1)} %bitcast.15, bf16[512,512]{1,0:T(8,128)(2,1)} %bitcast.17, bf16[512,1024]{1,0:T(8,128)(2,1)} %bitcast.13, bf16[512,512]{1,0:T(8,128)(2,1)} %bitcast.19, ...), custom_call_target="tpu_custom_call" | custom-call | flops 10000000000 | bytes 67108864 | tf_op jit(solution)/shard_map/main/pallas_call | solution.py:513
  139.6 0.0 copy-start.1
  139.6 0.0 copy-start
  139.6 2.0 %copy.15 = bf16[1,512,512]{2,1,0:T(8,128)(2,1)} copy(bf16[1,512,512]{2,1,0:T(8,128)(2,1)} %bitcast.10) | data formatting | bytes 1048576
  141.6 1.9 %copy.16 = bf16[1,512,512]{2,1,0:T(8,128)(2,1)} copy(bf16[1,512,512]{2,1,0:T(8,128)(2,1)} %bitcast.9) | data formatting | bytes 1048576
  143.5 0.0 copy-done.1
  143.5 1.0 copy.17
  144.4 0.0 copy-done
  144.4 1.0 copy.18
Async XLA Ops:
  139.6 3.9 %copy-start.1 = (bf16[512,1024]{1,0:T(8,128)(2,1)S(1)}, bf16[512,1024]{1,0:T(8,128)(2,1)}, u32[]{:S(2)}) copy-start(bf16[512,1024]{1,0:T(8,128)(2,1)} %get-tuple-element.22) | copy-start | bytes 3145732
  139.6 4.9 %copy-start = (f32[1024,256]{1,0:T(8,128)S(1)}, f32[1024,256]{1,0:T(8,128)}, u32[]{:S(2)}) copy-start(f32[1024,256]{1,0:T(8,128)} %get-tuple-element.31) | copy-start | bytes 3145732

commit v4 on v3

--- a/solution.py
+++ b/solution.py
@@ -86,26 +86,8 @@
     return dot(jnp.where(lower, 1.0, 0.0).astype(BF16), gates, NN)
 
 
-def states_kernel(n, peers, lens, q, k, v, gates, cot, weight, *outs):
-    grad_o, fwd_o, bwd_o, decay_o = outs[:4]
+def states_kernel(lens, q, k, v, gates, cot, weight, grad_o, fwd_o, bwd_o, decay_o):
     tokens = q.shape[0]
-    if len(outs) > 4:
-        cot_own, cot_send = outs[4:]
-        dp = lax.axis_index("dp")
-        columns = cot.shape[1] // (n * peers)
-
-        @pl.when(pl.program_id(0) == 0)
-        def _():
-            for c in range(n):
-                to = slice(c * columns, (c + 1) * columns)
-                for s in range(peers):
-                    start = (c * peers + lax.rem(dp + s, peers)) * columns
-                    part = cot[:, pl.ds(pl.multiple_of(start, columns), columns)]
-                    if s == 0:
-                        cot_own[:, to] = part
-                    else:
-                        cot_send[s - 1, :, to] = part.astype(F32)
-
     bounds = bounds_of(lens)
     first = lax.axis_index("ctx") * tokens
     grad = dot(cot[...], weight[...], NT)
@@ -120,14 +102,18 @@
     decay_o[...] = (jnp.exp(end) * living[tokens - 1 :, :])[None]
 
 
-def main_kernel(
-    n, peers, pieces, norm,
-    lens, q, k, v, gates, grad, fwd, bwd, decay, cot_own, cot_send,
-    q_o, k_o, v_o, out,
-    f_send, b_send, f_recv, b_recv, cum_s, attn_l, dq_l, dk_l, dv_l, fwd_c, bwd_c,
-    cot_in, attn, attn_in, part, line_in,
-    chain_sems, cot_sems, attn_send, attn_recv, line_send, line_recv,
-):
+def main_kernel(n, peers, pieces, norm, picks, *refs):
+    if picks:
+        refs = refs[:9] + refs[-2:] + refs[9:-2]
+        cot = refs[11]
+        refs = refs[:11] + refs[12:]
+    (
+        lens, q, k, v, gates, grad, fwd, bwd, decay, cot_own, cot_send,
+        q_o, k_o, v_o, out,
+        f_send, b_send, f_recv, b_recv, cum_s, attn_l, dq_l, dk_l, dv_l, fwd_c, bwd_c,
+        cot_in, attn, attn_in, part, line_in,
+        chain_sems, cot_sems, attn_send, attn_recv, line_send, line_recv,
+    ) = refs
     me, dp, mp = lax.axis_index("ctx"), lax.axis_index("dp"), lax.axis_index("mp")
     tokens = q.shape[0]
     heads = decay.shape[0]
@@ -168,8 +154,17 @@
             cot_sems.at[1, p, m + 1], {"mp": mates[m]},
         )
 
-    for p in range(peers - 1):
-        cot_copy(p).start()
+    def pick_columns():
+        width = cot_own.shape[1] // n
+        for c in range(n):
+            to = slice(c * width, (c + 1) * width)
+            for s in range(peers):
+                start = (c * peers + lax.rem(dp + s, peers)) * width
+                mine = cot[:, pl.ds(pl.multiple_of(start, width), width)]
+                if s == 0:
+                    cot_own[:, to] = mine
+                else:
+                    cot_send[s - 1, :, to] = mine.astype(F32)
 
     rows_each = fwd.shape[0] // pieces
     per_head = pieces // heads
@@ -290,30 +285,6 @@
                 keep = jnp.exp(end) * living[SPAN - 1 :, :]
                 state = keep * state + bwd_c[h, b - 1]
 
-    done, waiting = 0, [(h, b) for h in range(heads) for b in range(blocks)]
-    for h in range(heads):
-        target = (h + 1) * per_head + SKEW * (n - 1)
-        own = [u for u in waiting if u[0] <= h]
-        more = [u for u in waiting if u[0] > h][: blocks // 2]
-        waiting = [u for u in waiting if u not in own and u not in more]
-        start = done
-        for i, unit in enumerate(own + more):
-            until = start + (i + 1) * (target - start) // len(own + more)
-            lax.fori_loop(done, until, slot, 0)
-            done = until
-            inner(*unit)
-        lax.fori_loop(done, target, slot, 0)
-        done = target
-        forward(h)
-        for j in range(h * parts_of_head, (h + 1) * parts_of_head):
-            for p in range(peers - 1):
-                attn_copy(p, j).start()
-
-    for p in range(peers - 1):
-        cot_copy(p).wait_recv()
-        for m in range(cores - 1):
-            mate_copy(p, m).start()
-
     columns = out.shape[1]
     parts = attn.shape[0]
 
@@ -329,10 +300,6 @@
             part.at[j, 0], line_in.at[j, place], line_send.at[j, 0], line_recv.at[j, place],
             {"ctx": right if up else left},
         )
-
-    for p in range(peers - 1):
-        for m in range(cores - 1):
-            mate_copy(p, m).wait_recv()
 
     def multiply(j):
         total = dot(attn[j].astype(BF16), cot_own[...], TN)
@@ -347,26 +314,36 @@
             part.at[j, c], line_in.at[j, c], line_send.at[j, c], line_recv.at[j, c], {"ctx": right}
         )
 
-    def add_and_send(j, c, up, has_source):
-        @pl.when(has_source)
-        def _():
-            arrival(j, c, up).wait_recv()
-            part[j, c] = part[j, c] + line_in[j, c]
-
+    def send_off(j):
+        for c in reversed(range(1, n)):
+
+            @pl.when(me == 0)
+            def _():
+                line_copy(j, c, True).start()
+
+        for c in range(n - 1):
+
+            @pl.when(me == n - 1)
+            def _():
+                line_copy(j, c, False).start()
+
+    def add_and_send(j, c, up):
+        arrival(j, c, up).wait_recv()
+        part[j, c] = part[j, c] + line_in[j, c]
         line_copy(j, c, up).start()
 
     def pass_on(j):
         for c in reversed(range(1, n)):
 
-            @pl.when(me < c)
+            @pl.when((me < c) & has_left)
             def _():
-                add_and_send(j, c, True, has_left)
+                add_and_send(j, c, True)
 
         for c in range(n - 1):
 
-            @pl.when(me > c)
+            @pl.when((me > c) & has_right)
             def _():
-                add_and_send(j, c, False, has_right)
+                add_and_send(j, c, False)
 
     def settle(j):
         at = pl.ds(j * PIECE, PIECE)
@@ -382,11 +359,51 @@
             arrival(j, n, False).wait_recv()
             out[at, :] = out[at, :] + line_in[j, n] * norm
 
-    for j in range(parts):
+    def send_head(h):
+        forward(h)
+        for j in range(h * parts_of_head, (h + 1) * parts_of_head):
+            for p in range(peers - 1):
+                attn_copy(p, j).start()
+
+    def slots_with(first, last, units):
+        done = first
+        for i, unit in enumerate(units):
+            until = first + (i + 1) * (last - first) // len(units)
+            lax.fori_loop(done, until, slot, 0)
+            done = until
+            inner(*unit)
+        lax.fori_loop(done, last, slot, 0)
+
+    begun, through = 3, per_head + SKEW * (n - 1)
+    lax.fori_loop(0, begun, slot, 0)
+    if picks:
+        pick_columns()
+    for p in range(peers - 1):
+        cot_copy(p).start()
+    slots_with(begun, through, [(0, b) for b in range(blocks)])
+    send_head(0)
+    later = [(h, b) for h in range(1, heads) for b in range(blocks)]
+    slots_with(through, pieces + SKEW * (n - 1), later[: blocks // 2])
+    for p in range(peers - 1):
+        cot_copy(p).wait_recv()
+        for m in range(cores - 1):
+            mate_copy(p, m).start()
+    for p in range(peers - 1):
+        for m in range(cores - 1):
+            mate_copy(p, m).wait_recv()
+    multiply(0)
+    send_off(0)
+    for unit in later[blocks // 2 :]:
+        inner(*unit)
+    for h in range(1, heads):
+        send_head(h)
+    pass_on(0)
+    for j in range(1, parts):
         multiply(j)
+        send_off(j)
         pass_on(j)
-        if j < heads:
-            backward(j)
+        if j <= heads:
+            backward(j - 1)
     for j in range(parts):
         settle(j)
 
@@ -438,8 +455,8 @@
     def head_rows(rows, cols):
         return pl.BlockSpec((rows, cols), lambda h: (h, 0))
 
-    grad, fwd, bwd, decay, *cots = pl.pallas_call(
-        functools.partial(states_kernel, n, peers),
+    grad, fwd, bwd, decay = pl.pallas_call(
+        states_kernel,
         grid=(heads,),
         in_specs=[
             smem,
@@ -455,30 +472,20 @@
             head_rows(VAL, KEY),
             head_rows(VAL, KEY),
             pl.BlockSpec((1, 1, KEY), lambda h: (h, 0, 0)),
-        ]
-        + [
-            pl.BlockSpec((tokens, spread), lambda h: (0, 0)),
-            pl.BlockSpec((peers - 1, tokens, spread), lambda h: (0, 0, 0)),
-        ]
-        * in_kernel,
+        ],
         out_shape=[
             jax.ShapeDtypeStruct((tokens, heads * VAL), F32),
             jax.ShapeDtypeStruct((heads * VAL, KEY), F32),
             jax.ShapeDtypeStruct((heads * VAL, KEY), F32),
             jax.ShapeDtypeStruct((heads, 1, KEY), F32),
-        ]
-        + [
-            jax.ShapeDtypeStruct((tokens, spread), BF16),
-            jax.ShapeDtypeStruct((peers - 1, tokens, spread), F32),
-        ]
-        * in_kernel,
+        ],
         compiler_params=params(),
         cost_estimate=pl.CostEstimate(flops=6 * 10**9, bytes_accessed=14 << 20, transcendentals=0),
         name="states",
     )(doc_lengths, q, k, v, gates, cot, out_weight)
 
     if in_kernel:
-        cot_own, cot_send = cots
+        cots = [cot]
     else:
         parted = cot.reshape(tokens, n, peers, columns)
         shares = [
@@ -487,7 +494,7 @@
             )
             for s in range(peers)
         ]
-        cot_own, cot_send = shares[0], jnp.stack(shares[1:]).astype(F32)
+        cots = [shares[0], jnp.stack(shares[1:]).astype(F32)]
 
     pieces = 8 * heads
     vmem = pl.BlockSpec(memory_space=pltpu.VMEM)
@@ -511,8 +518,8 @@
         ]
     )
     query_grad, key_grad, value_grad, weight_grad = pl.pallas_call(
-        functools.partial(main_kernel, n, peers, pieces, norm),
-        in_specs=[smem] + [vmem] * 10,
+        functools.partial(main_kernel, n, peers, pieces, norm, in_kernel),
+        in_specs=[smem] + [vmem] * (8 + len(cots)),
         out_specs=[vmem] * 4,
         out_shape=[
             jax.ShapeDtypeStruct(keys, BF16),
@@ -528,11 +535,13 @@
             dma((peers - 1, parts)),
             dma((parts, n)),
             dma((parts, n + 1)),
-        ],
+        ]
+        + [pltpu.VMEM((tokens, spread), BF16), pltpu.VMEM((peers - 1, tokens, spread), F32)]
+        * in_kernel,
         compiler_params=params(collective_id=0, has_side_effects=True),
         cost_estimate=pl.CostEstimate(flops=10**10, bytes_accessed=64 << 20, transcendentals=0),
         name="main",
-    )(doc_lengths, q, k, v, gates, grad, fwd, bwd, decay, cot_own, cot_send)
+    )(doc_lengths, q, k, v, gates, grad, fwd, bwd, decay, *cots)
     return (query_grad[None], key_grad[None], value_grad[None], weight_grad)
 
 

time: 146 us -> 144 us (0.986)
  Pallas kernels: 139 us -> 137 us
    pallas_call x2, Pallas kernels: 139 us -> 137 us  [the longest x1 128 us: per_device(): pl.pallas_call(functools.partial(main_kernel, n, peers, pieces, norm, in_...]
where the time goes in v4:
time: 144 us; the launch traced here: 143 us
  Pallas kernels  137 us (95%)
  local copies, waits for them, and re-layouts  5.83 us (4%)
    pallas_call x1, Pallas kernels, per_device(): pl.pallas_call(functools.partial(main_kernel, n, peers, pieces, norm, in_...  128 us
    pallas_call x1, Pallas kernels, per_device(): pl.pallas_call(states_kernel, grid=(heads,), in_specs=[smem, head_block(t...  8.97 us
    unnamed x8, local copies, waits for them, and re-layouts  5.83 us

profile of v4, /device:TPU:0, one launch (start us, length us, event | category | flops | bytes accessed | tf_op | source)
XLA Modules:
  0.0 143.4 jit_solution(5157734988291516575)
XLA Ops:
  0.6 9.0 %states.1 = (f32[512,1024]{1,0:T(8,128)}, f32[1024,256]{1,0:T(8,128)}, f32[1024,256]{1,0:T(8,128)}, f32[2,1,256]{2,1,0:T(1,128)}) custom-call(s32[1,6]{1,0:T(1,128)} %refs_0_.1, bf16[512,512]{1,0:T(8,128)(2,1)} %bitcast.15, bf16[512,512]{1,0:T(8,128)(2,1)} %bitcast.17, bf16[512,1024]{1,0:T(8,128)(2,1)} %bitcast.13, bf16[512,512]{1,0:T(8,128)(2,1)} %bitcast.19, ...), custom_call_target="tpu_custom_call" | custom-call | flops 6000000000 | bytes 14680064 | tf_op jit(solution)/shard_map/states/pallas_call | solution.py:458
  9.6 127.9 %main.1 = (bf16[512,512]{1,0:T(8,128)(2,1)}, bf16[512,512]{1,0:T(8,128)(2,1)}, bf16[512,1024]{1,0:T(8,128)(2,1)}, f32[1024,256]{1,0:T(8,128)}) custom-call(s32[1,6]{1,0:T(1,128)} %refs_0_.1, bf16[512,512]{1,0:T(8,128)(2,1)} %bitcast.16, bf16[512,512]{1,0:T(8,128)(2,1)} %bitcast.18, bf16[512,1024]{1,0:T(8,128)(2,1)} %bitcast.14, bf16[512,512]{1,0:T(8,128)(2,1)} %bitcast.20, ...), custom_call_target="tpu_custom_call" | custom-call | flops 10000000000 | bytes 67108864 | tf_op jit(solution)/shard_map/main/pallas_call | solution.py:520
  137.5 0.0 copy-start.1
  137.5 0.0 copy-start
  137.5 2.0 %copy.15 = bf16[1,512,512]{2,1,0:T(8,128)(2,1)} copy(bf16[1,512,512]{2,1,0:T(8,128)(2,1)} %bitcast.10) | data formatting | bytes 1048576
  139.5 1.9 %copy.16 = bf16[1,512,512]{2,1,0:T(8,128)(2,1)} copy(bf16[1,512,512]{2,1,0:T(8,128)(2,1)} %bitcast.9) | data formatting | bytes 1048576
  141.4 0.0 copy-done.1
  141.4 1.0 copy.17
  142.4 0.0 copy-done
  142.4 1.0 copy.18
Async XLA Ops:
  137.5 3.9 %copy-start.1 = (bf16[512,1024]{1,0:T(8,128)(2,1)S(1)}, bf16[512,1024]{1,0:T(8,128)(2,1)}, u32[]{:S(2)}) copy-start(bf16[512,1024]{1,0:T(8,128)(2,1)} %get-tuple-element.18) | copy-start | bytes 3145732
  137.5 4.9 %copy-start = (f32[1024,256]{1,0:T(8,128)S(1)}, f32[1024,256]{1,0:T(8,128)}, u32[]{:S(2)}) copy-start(f32[1024,256]{1,0:T(8,128)} %get-tuple-element.27) | copy-start | bytes 3145732
